TPU v7x, 256 devices: a whole 4x4x8 slice. The times are simulated.
256 devices in a mesh: qb: 32 (over y_lo, z, core), kb: 8 (over x, y_hi).
Axes of the slice: x: 4, y: 4 (y_hi: 2, y_lo: 2; y = y_hi * 2 + y_lo), z: 8, core: 2. Of those that a mesh axis runs over, the one named last changes fastest.
Arguments:
- queries: bfloat16 [4, 16384, 128], P(None, 'qb'), may hold values from -100 to 100
- keys: bfloat16 [4, 16384, 128], P(None, ('qb', 'kb')), may hold values from -3.5 to 3.5
- c_proj: bfloat16 [4, 16384, 128], P(None, 'qb'), may hold values from -0.5 to 0.5
- b_proj: bfloat16 [4, 16384, 128], P(None, ('qb', 'kb')), may hold values from -0.5 to 0.5
- decay_rate: float32 [4, 16384], replicated, may hold values from 0 to 1
- doc_ids: int32 [4, 128], replicated, may hold values from 0 to 7, never falling along the last dimension, each value on 1 to 48 neighbouring positions
Outputs:
- grad_c: float32 [4, 16384, 128], P(None, ('qb', 'kb'))
- grad_b: float32 [4, 16384, 128], P(None, ('qb', 'kb'))
- grad_logcum: float32 [4, 16384], P(None, ('qb', 'kb'))
Inputs may be any that keep to these rules, and one draw needn't show every extreme that they name: `doc_ids`: within a sequence the numbers never fall; a document covers 1 to 48 blocks.
All inputs are finite; a program needn't handle non-finite values.
Results may differ from a plain program's by a relative error of at most 0.00068.
Values may be sent and summed in bfloat16 or wider, within the bound.
A program may use at most 128 MiB of HBM per device.

v0:
```python
import jax
import jax.numpy as jnp
from jax import lax
from jax.sharding import PartitionSpec as P

NEGATIVE = -1e30


def merged(part, axis, combine):
    gathered = jax.tree.map(lambda a: lax.all_gather(a, axis), part)

    def take(source):
        return jax.tree.map(lambda a: lax.dynamic_index_in_dim(a, source, 0, False), gathered)

    return lax.fori_loop(
        1, lax.axis_size(axis), lambda source, state: combine(state, take(source)), take(0)
    )


def merge_stats(first, second):
    joined = jnp.maximum(first[0], second[0])
    summed = first[1] * jnp.exp(first[0] - joined) + second[1] * jnp.exp(second[0] - joined)
    return (joined, summed)


def tile_mask(row_pos, row_doc, key_pos, key_doc):
    return (key_pos[None, None, :] <= row_pos[None, :, None]) & (
        key_doc[:, None, :] == row_doc[:, :, None]
    )


def tile_active(row_pos, row_doc, key_pos, key_doc):
    reach = (key_pos[None, :] <= row_pos[-1]) & (
        (key_pos[None, :] >= row_pos[0]) | (key_doc == row_doc[:, :1])
    )
    return jnp.any(reach)


def shards(queries, keys, c_proj, b_proj, decay_rate, doc_ids):
    query_count = lax.axis_size("qb")
    key_count = lax.axis_size("kb")
    query_index = lax.axis_index("qb")
    key_index = lax.axis_index("kb")
    sequences, row_count, head_width = queries.shape
    shard_rows = keys.shape[1]
    half_rows = row_count // 2
    key_total = shard_rows * query_count
    part_keys = key_total // 4
    score_scale = head_width ** (-0.5)
    logcum = jnp.cumsum(-decay_rate, axis=1)
    documents = jnp.repeat(doc_ids, 128, axis=1)
    seq_len = documents.shape[1]
    positions = jnp.arange(seq_len, dtype=jnp.int32)
    key_rows, bproj_rows = (
        lax.all_gather(keys, "qb", axis=1, tiled=True),
        lax.all_gather(b_proj, "qb", axis=1, tiled=True),
    )

    def key_side(values):
        grid = values.reshape(values.shape[:-1] + (query_count, key_count, shard_rows))
        picked = lax.dynamic_index_in_dim(grid, key_index, grid.ndim - 2, keepdims=False)
        return picked.reshape(values.shape[:-1] + (key_total,))

    key_pos = key_side(positions)
    key_cum = key_side(logcum)
    key_doc = key_side(documents)
    starts = (2 * query_index * half_rows, (2 * query_index + 1) * half_rows)
    halves = []
    for half_part in range(2):
        begin = starts[half_part]
        halves.append(
            (
                queries[:, half_part * half_rows : (half_part + 1) * half_rows],
                c_proj[:, half_part * half_rows : (half_part + 1) * half_rows],
                begin + jnp.arange(half_rows, dtype=jnp.int32),
                lax.dynamic_slice_in_dim(logcum, begin, half_rows, 1),
                lax.dynamic_slice_in_dim(documents, begin, half_rows, 1),
            )
        )
    parts = []
    for key_part in range(4):
        first_key = key_part * part_keys
        parts.append(
            (
                key_rows[:, first_key : first_key + part_keys],
                bproj_rows[:, first_key : first_key + part_keys],
                key_pos[first_key : first_key + part_keys],
                key_cum[:, first_key : first_key + part_keys],
                key_doc[:, first_key : first_key + part_keys],
            )
        )
    actives = [
        [
            tile_active(
                halves[half_part][2], halves[half_part][4], parts[key_part][2], parts[key_part][4]
            )
            for key_part in range(4)
        ]
        for half_part in range(2)
    ]
    top_parts = []
    total_parts = []
    stored = []
    for half_part in range(2):
        query_half, cproj_half, row_pos, row_cum, row_doc = halves[half_part]
        running = (
            jnp.full((sequences, half_rows), NEGATIVE, jnp.float32),
            jnp.zeros((sequences, half_rows), jnp.float32),
        )
        stored_half = []
        for key_part in range(4):
            key_block, bproj_block, block_pos, block_cum, block_doc = parts[key_part]

            def visit_stats(carry):
                scores = (
                    jnp.einsum(
                        "srd,skd->srk", query_half, key_block, preferred_element_type=jnp.float32
                    )
                    * score_scale
                )
                allowed = tile_mask(row_pos, row_doc, block_pos, block_doc)
                masked = jnp.where(allowed, scores, NEGATIVE)
                local_top = jnp.max(masked, axis=2)
                local_sum = jnp.sum(
                    jnp.where(allowed, jnp.exp(masked - local_top[:, :, None]), 0.0), axis=2
                )
                return (merge_stats(carry, (local_top, local_sum)), masked)

            def pass_stats(carry):
                return (carry, jnp.full((sequences, half_rows, part_keys), NEGATIVE, jnp.float32))

            running, masked = lax.cond(
                actives[half_part][key_part], visit_stats, pass_stats, running
            )
            stored_half.append(masked)
        stored.append(stored_half)
        top_parts.append(running[0])
        total_parts.append(running[1])
    row_top, row_total = merged(
        (jnp.concatenate(top_parts, axis=1), jnp.concatenate(total_parts, axis=1)),
        "kb",
        merge_stats,
    )
    grad_c_halves = []
    row_flow_halves = []
    grad_b_parts = [
        jnp.zeros((sequences, part_keys, head_width), jnp.float32) for key_part in range(4)
    ]
    col_flow_parts = [jnp.zeros((sequences, part_keys), jnp.float32) for key_part in range(4)]
    for half_part in range(2):
        query_half, cproj_half, row_pos, row_cum, row_doc = halves[half_part]
        top_half = row_top[:, half_part * half_rows : (half_part + 1) * half_rows]
        total_half = row_total[:, half_part * half_rows : (half_part + 1) * half_rows]
        grad_c_acc = jnp.zeros((sequences, half_rows, head_width), jnp.float32)
        row_flow_acc = jnp.zeros((sequences, half_rows), jnp.float32)
        for key_part in range(4):
            key_block, bproj_block, block_pos, block_cum, block_doc = parts[key_part]
            masked = stored[half_part][key_part]

            def visit_grads(state):
                cgrad_acc, rflow_acc, bgrad_acc, cflow_acc = state
                allowed = tile_mask(row_pos, row_doc, block_pos, block_doc)
                attention = jnp.where(
                    allowed, jnp.exp(masked - top_half[:, :, None]) / total_half[:, :, None], 0.0
                )
                products = jnp.einsum(
                    "srd,skd->srk", cproj_half, bproj_block, preferred_element_type=jnp.float32
                )
                spread = jnp.where(allowed, row_cum[:, :, None] - block_cum[:, None, :], 0.0)
                decay_tile = jnp.where(allowed, jnp.exp(spread), 0.0)
                mixing = products * decay_tile
                twice_gap = jnp.where(allowed, 2.0 * (mixing - attention), 0.0)
                weighted = (twice_gap * decay_tile).astype(jnp.bfloat16)
                flow_tile = twice_gap * mixing
                return (
                    cgrad_acc
                    + jnp.einsum(
                        "srk,skd->srd", weighted, bproj_block, preferred_element_type=jnp.float32
                    ),
                    rflow_acc + jnp.sum(flow_tile, axis=2),
                    bgrad_acc
                    + jnp.einsum(
                        "srk,srd->skd", weighted, cproj_half, preferred_element_type=jnp.float32
                    ),
                    cflow_acc + jnp.sum(flow_tile, axis=1),
                )

            def keep_state(state):
                return state

            grad_c_acc, row_flow_acc, grad_b_parts[key_part], col_flow_parts[key_part] = lax.cond(
                actives[half_part][key_part],
                visit_grads,
                keep_state,
                (grad_c_acc, row_flow_acc, grad_b_parts[key_part], col_flow_parts[key_part]),
            )
        grad_c_halves.append(grad_c_acc)
        row_flow_halves.append(row_flow_acc)
    grad_b, col_share = (
        lax.psum_scatter(
            jnp.concatenate(grad_b_parts, axis=1), "qb", scatter_dimension=1, tiled=True
        ),
        lax.psum_scatter(
            jnp.concatenate(col_flow_parts, axis=1), "qb", scatter_dimension=1, tiled=True
        ),
    )
    grad_c, row_share = (
        lax.psum_scatter(
            jnp.concatenate(grad_c_halves, axis=1), "kb", scatter_dimension=1, tiled=True
        ),
        lax.psum_scatter(
            jnp.concatenate(row_flow_halves, axis=1), "kb", scatter_dimension=1, tiled=True
        ),
    )
    return (grad_c, grad_b, row_share - col_share)


def solution(mesh):
    placed = (
        P(None, "qb", None),
        P(None, ("qb", "kb"), None),
        P(None, "qb", None),
        P(None, ("qb", "kb"), None),
        P(),
        P(),
    )
    return jax.shard_map(
        shards,
        mesh=mesh,
        in_specs=placed,
        out_specs=(P(None, ("qb", "kb"), None), P(None, ("qb", "kb"), None), P(None, ("qb", "kb"))),
        check_vma=False,
    )
```

profile of v0, /device:TPU:1, one launch (start us, length us, event | category | flops | bytes accessed | tf_op | source)
XLA Modules:
  0.0 631.8 jit_solution(11352791467986797202)
XLA Ops:
  7.2 0.7 all-gather.9.cloned.1.call-update
  8.0 0.7 all-gather.7.cloned.1.call-update
  8.7 1.0 negate_bitcast_fusion
  9.9 0.3 reduce-window.6
  10.2 0.3 reduce-window.9
  11.1 0.2 copy.68
  11.2 0.2 fusion.18
  11.5 0.6 fusion.37
  12.1 0.6 fusion.36
  13.4 0.3 copy.47
  14.3 0.3 fusion.16
  14.6 2.6 broadcast_compare_fusion.30
  17.2 2.6 broadcast_compare_fusion.28
  19.8 0.8 and_reduce_fusion
  23.1 0.8 and_reduce_fusion.5
  26.7 0.8 fusion.30
  27.4 51.4 %all-gather.9.cloned.1.call-done = bf16[4,2048,128]{2,1,0:T(8,128)(2,1)} async-done(((bf16[4,64,128]{2,1,0:T(8,128)(2,1)}), bf16[4,2048,128]{2,1,0:T(8,128)(2,1)}) %all-gather.9.cloned.1.call-update) | async-done | bytes 2097168 | tf_op jit(solution)/shard_map/all_gather | solution.py:55
  78.9 1.7 fusion.29
  80.5 4.7 conditional.20
  80.7 2.0 fusion.27
  82.7 2.6 select_reduce_fusion.4
  85.3 4.7 conditional.16
  85.4 2.0 fusion.26
  87.4 2.6 select_reduce_fusion
  90.0 1.6 conditional.21
  90.0 1.6 broadcast.639
  91.6 1.6 conditional.17
  91.6 1.6 broadcast.627
  93.2 1.7 conditional.22
  93.2 1.6 broadcast.641
  95.0 1.6 conditional.18
  95.0 1.6 broadcast.629
  96.6 1.6 conditional.23
  96.6 1.6 broadcast.643
  98.2 1.7 conditional.19
  98.2 1.7 broadcast.631
  99.9 28.1 %all-gather.3 = f32[8,4,512]{2,1,0:T(4,128)S(1)} all-gather(f32[1,4,512]{2,1,0:T(4,128)S(1)} %maximum_bitcast_fusion.1), channel_id=3, replica_groups=mesh['qb'=32,'kb'=8] {'kb'}, dimensions={0}, use_global_device_ids=true | all-gather | bytes 73728 | tf_op jit(solution)/shard_map/all_gather | solution.py:10
  128.0 28.0 %all-gather.2 = f32[8,4,512]{2,1,0:T(4,128)S(1)} all-gather(f32[1,4,512]{2,1,0:T(4,128)S(1)} %maximum_bitcast_fusion), channel_id=2, replica_groups=mesh['qb'=32,'kb'=8] {'kb'}, dimensions={0}, use_global_device_ids=true | all-gather | bytes 73728 | tf_op jit(solution)/shard_map/all_gather | solution.py:10
  156.0 0.3 while.17
  156.4 2.7 fusion.28
  159.1 6.6 %conditional.24 = (f32[4,256,128]{2,1,0:T(8,128)}, f32[4,256]{1,0:T(4,128)S(1)}, f32[4,512,128]{2,1,0:T(8,128)S(1)}, f32[4,512]{1,0:T(4,128)S(1)}) conditional(s32[]{:T(128)} %convert_element_type.59, () %tuple.155, (s32[512]{0:T(512)S(1)}, s32[256]{0:T(256)S(1)}, s32[4,512]{1,0:T(4,128)S(1)}, s32[4,256]{1,0:T(4,128)S(1)}, ...), branch_computations={%region_44.45_spmd, %region_45.48_spmd} | conditional | flops 417985536 | bytes 12155936 | solution.py:191
  159.2 3.2 multiply_reduce_fusion
  162.5 1.9 fusion.4
  164.3 1.3 fusion.3
  165.7 0.3 conditional.25
  166.0 10.7 %conditional.28 = (f32[4,256,128]{2,1,0:T(8,128)}, f32[4,256]{1,0:T(4,128)S(1)}, f32[4,512,128]{2,1,0:T(8,128)S(1)}, f32[4,512]{1,0:T(4,128)S(1)}) conditional(s32[]{:T(128)} %convert_element_type.63, (f32[4,512,128]{2,1,0:T(8,128)S(1)}, f32[4,512]{1,0:T(4,128)S(1)}) %tuple.180, (s32[512]{0:T(512)S(1)}, s32[256]{0:T(256)S(1)}, ...), branch_computations={%region_60.61_spmd, %region_61.64_spmd} | conditional | flops 424541184 | bytes 17439776 | solution.py:191
  166.2 3.2 multiply_reduce_fusion.8
  169.4 3.4 convolution_add_fusion.3
  172.8 4.0 fusion.12
  176.8 0.4 conditional.29
  177.3 1.1 conditional.27
  177.3 1.1 broadcast.656
  178.4 3.3 conditional.31
  181.7 0.9 copy.56
  182.6 1.4 copy.58
  184.1 2.2 pad_maximum_fusion.1
  186.4 3.5 pad_maximum_fusion
  189.9 117.0 %reduce-scatter.13.cloned.1.call-done = f32[64,4]{1,0:T(8,128)} async-done(((f32[512,4]{1,0:T(8,128)}), f32[64,4]{1,0:T(8,128)}) %reduce-scatter.13.cloned.1.call-update) | async-done | bytes 1040
  306.9 0.8 copy.57
  307.8 115.7 %reduce-scatter.15.cloned.1.call-done = f32[64,4]{1,0:T(8,128)} async-done(((f32[2048,4]{1,0:T(8,128)}), f32[64,4]{1,0:T(8,128)}) %reduce-scatter.15.cloned.1.call-update) | async-done | bytes 1040
  423.4 0.8 copy.59
  424.3 0.6 sub.327
  424.9 77.8 %reduce-scatter.9.cloned.1.call-done = f32[4,64,128]{2,1,0:T(8,128)} async-done(((f32[4,512,128]{2,1,0:T(8,128)}), f32[4,64,128]{2,1,0:T(8,128)}) %reduce-scatter.9.cloned.1.call-update) | async-done | bytes 131088 | tf_op jit(solution)/shard_map/reduce_scatter | solution.py:208
  502.7 122.1 %reduce-scatter.11.cloned.1.call-done = f32[4,64,128]{2,1,0:T(8,128)} async-done(((f32[4,2048,128]{2,1,0:T(8,128)}), f32[4,64,128]{2,1,0:T(8,128)}) %reduce-scatter.11.cloned.1.call-update) | async-done | bytes 131088 | tf_op jit(solution)/shard_map/reduce_scatter | solution.py:200
  (83 shorter events, 3.5 us)
Async XLA Ops:
  7.2 3.6 copy-start.13
  7.2 71.7 %all-gather.9.cloned.1.call-start = ((), (), s32[]{:S(2)}) async-start(), calls=%async_computation.5 | async-start | bytes 2162688 | tf_op jit(solution)/shard_map/all_gather | solution.py:55
  7.9 148.5 %all-gather.7.cloned.1.call-start = ((), (), s32[]{:S(2)}) async-start(), calls=%async_computation.4 | async-start | bytes 2162688 | tf_op jit(solution)/shard_map/all_gather | solution.py:56
  8.7 298.3 %reduce-scatter.13.cloned.1.call-start = ((), (), s32[]{:S(2)}) async-start(), calls=%async_computation.8 | async-start | bytes 294912
  10.9 15.7 %copy-start = (bf16[4,512,128]{2,1,0:T(8,128)(2,1)S(1)}, bf16[4,512,128]{2,1,0:T(8,128)(2,1)}, u32[]{:S(2)}) copy-start(bf16[4,512,128]{2,1,0:T(8,128)(2,1)} %param.40) | copy-start | bytes 1572868
  13.2 13.5 %copy-start.1 = (bf16[4,512,128]{2,1,0:T(8,128)(2,1)S(1)}, bf16[4,512,128]{2,1,0:T(8,128)(2,1)}, u32[]{:S(2)}) copy-start(bf16[4,512,128]{2,1,0:T(8,128)(2,1)} %param.42) | copy-start | bytes 1572868
  156.3 2.8 copy-start.8
  159.1 6.6 %copy-start.6 = (bf16[4,512,128]{2,1,0:T(8,128)(2,1)}, bf16[4,512,128]{2,1,0:T(8,128)(2,1)S(1)}, u32[]{:S(2)}) copy-start(bf16[4,512,128]{2,1,0:T(8,128)(2,1)S(1)} %get-tuple-element.922) | copy-start | bytes 1572868
  182.6 240.9 %reduce-scatter.15.cloned.1.call-start = ((), (), s32[]{:S(2)}) async-start(), calls=%async_computation.9 | async-start | bytes 1081344
  184.0 318.7 %reduce-scatter.9.cloned.1.call-start = ((), (), s32[]{:S(2)}) async-start(), calls=%async_computation.6 | async-start | bytes 1179648 | tf_op jit(solution)/shard_map/reduce_scatter | solution.py:208
  186.4 438.4 %reduce-scatter.11.cloned.1.call-start = ((), (), s32[]{:S(2)}) async-start(), calls=%async_computation.7 | async-start | bytes 4325376 | tf_op jit(solution)/shard_map/reduce_scatter | solution.py:200
Sparse Core Ops, SparseCore 0:
  9.9 68.9 all-gather.8
  80.7 64.2 all-gather.6
  182.7 124.2 reduce-scatter.12
  309.4 113.9 reduce-scatter.14
  427.8 74.8 reduce-scatter.8
  505.8 118.8 reduce-scatter.10
where the time goes:
time: 644 us; the launch traced here: 632 us
  waiting for transfers between devices  485 us (75%)
  blocking collectives  56.1 us (9%)
  local copies, waits for them, and re-layouts  23.9 us (4%)
  other arithmetic  20.9 us (3%)
  matrix products  20.9 us (3%)
  between operations  19.9 us (3%)
    unnamed x8, waiting for transfers between devices  234 us
    reduce_scatter x1, waiting for transfers between devices, shards(): lax.psum_scatter(jnp.concatenate(grad_b_parts, axis=1), 'qb', scatter_dim...  122 us
    reduce_scatter x1, waiting for transfers between devices, shards(): lax.psum_scatter(jnp.concatenate(grad_c_halves, axis=1), 'kb', scatter_di...  77.8 us
    all_gather x2, blocking collectives, merged(): gathered = jax.tree.map(lambda a: lax.all_gather(a, axis), part)  56.1 us
    all_gather x1, waiting for transfers between devices, shards(): lax.all_gather(keys, 'qb', axis=1, tiled=True)  51.4 us
  transfers between devices with their start and end apart: 6, of which 5 were waited for; matrix products, arithmetic and copies ran while one was open for 7% of the time, Pallas kernels for 0%

commit v1 on v0

v1 whole, which is shorter than its diff:
```python
import functools
import math

import jax
import jax.numpy as jnp
from jax import lax
from jax.experimental import pallas as pl
from jax.experimental.pallas import tpu as pltpu
from jax.sharding import PartitionSpec as P

MESH = pl.DeviceIdType.MESH
NEG = -1e30
SK = 64
BLK = 128
SLOTS = 7


def nt(a, b, precision=None):
    return lax.dot_general(
        a, b, (((1,), (1,)), ((), ())), preferred_element_type=jnp.float32, precision=precision
    )


def kernel(
    nq, nk,
    q_ref, c_ref, k_ref, b_ref, lc_ref, doc_ref,
    gc_ref, gb_ref, gl_ref,
    kbuf, bbuf, ebuf, mbuf, lbuf, fbuf, lckb, gct, rf, gp, sib, up, dn, gcp, gcr, st, str_, cf,
    ks, kr, bs, br, kss, ksr, bss, bsr, sts, strs, gss, gsr, us, ur, ds, dr, gcs, gcrs,
):
    S, R, D = q_ref.shape
    RB = R // BLK
    NROW = S * SK
    npair = nq // 2
    qb = lax.axis_index("qb")
    kb = lax.axis_index("kb")
    pr = qb // 2
    core = qb % 2
    other = 1 - core
    kblk = (kb * SK) // BLK
    khalf = kb % 2

    def dev(step):
        return (((pr + step + npair) % npair) * 2 + core, kb)

    nxt, prv, far, back = dev(1), dev(-1), dev(6), dev(-6)
    sibling = (pr * 2 + other, kb)
    peers = [(qb, (kb + o) % nk) for o in range(1, nk)]

    def rc(src, dst, ssem, rsem, to):
        return pltpu.make_async_remote_copy(
            src_ref=src, dst_ref=dst, send_sem=ssem, recv_sem=rsem, device_id=to, device_id_type=MESH
        )

    def ring(own, buf, ssem, rsem):
        def src(e):
            return own if e == 0 else buf.at[e, :, core]

        plan = {1: (0, nxt), 2: (1, nxt), 3: (2, nxt), 6: (0, far), 5: (6, prv), 4: (5, prv)}
        return {e: rc(src(f), buf.at[e, :, core], ssem.at[e], rsem.at[e], to) for e, (f, to) in plan.items()}

    def pair_up(own, buf, ssem, rsem):
        out = []
        for e in range(SLOTS):
            src = own if e == 0 else buf.at[e, :, core]
            out.append((
                rc(src, buf.at[e, :, core], ssem.at[e], rsem.at[e], sibling),
                rc(buf.at[e, :, other], buf.at[e, :, other], ssem.at[e], rsem.at[e], sibling),
            ))
        return out

    kc = ring(k_ref, kbuf, ks, kr)
    bc = ring(b_ref, bbuf, bs, br)
    kx = pair_up(k_ref, kbuf, kss, ksr)
    bx = pair_up(b_ref, bbuf, bss, bsr)

    barrier = pltpu.get_barrier_semaphore()
    partners = [nxt, prv, far, back, sibling] + peers
    for to in partners:
        pl.semaphore_signal(barrier, inc=1, device_id=to, device_id_type=MESH)
    pl.semaphore_wait(barrier, len(partners))

    kc[1].start()
    kc[6].start()
    kx[0][0].start()

    lane = lax.broadcasted_iota(jnp.int32, (1, BLK), 1)
    sub = lax.broadcasted_iota(jnp.int32, (BLK, BLK), 0)

    def key_block(e, u):
        j = (pr - e + npair) % npair
        return (2 * j + u) * RB + kblk

    def biases(e, s, r):
        rd = doc_ref[s, qb * RB + r]
        out = []
        for u in range(2):
            kd = doc_ref[s, key_block(e, u)]
            same = kd == rd
            if e:
                same = same & (pr >= e)
            out.append(jnp.where(same, 0.0, NEG).astype(jnp.float32))
        return out

    def causal(r):
        kpos = (2 * pr) * R + kb * SK + jnp.where(sub >= SK, sub - SK + R, sub)
        rpos = qb * R + r * BLK + lane
        return kpos <= rpos

    kbuf[0, :, core] = k_ref[...]
    bbuf[0, :, core] = b_ref[...]
    gct[...] = jnp.zeros_like(gct)
    rf[...] = jnp.zeros_like(rf)
    gp[:, :, NROW:, :] = jnp.zeros((SLOTS, 2, 8, D), jnp.float32)
    gcp[:, NROW:, :] = jnp.zeros((nk, 8, D), jnp.float32)

    def key_columns(e):
        def body(s, _):
            first = lc_ref[s, pl.ds(key_block(e, 0), 1), :]
            second = lc_ref[s, pl.ds(key_block(e, 1), 1), :]
            low = jnp.concatenate([first[:, :SK], second[:, :SK]], axis=1)
            high = jnp.concatenate([first[:, SK:], second[:, SK:]], axis=1)
            row = jnp.where(jnp.full((1, BLK), khalf) == 0, low, high)
            lckb[e, s] = jnp.broadcast_to(row, (BLK, BLK)).T
            return 0

        lax.fori_loop(0, S, body, 0)

    scale = (D ** -0.5) * math.log2(math.e)

    def first_pass(e):
        def body(s, _):
            keys = kbuf[e, s].reshape(BLK, D)
            for r in range(RB):
                cols = slice(r * BLK, (r + 1) * BLK)
                sc = nt(keys, q_ref[s, cols, :]) * scale
                if e == 0:
                    sc = jnp.where(causal(r), sc, NEG)
                bias = biases(e, s, r)
                halves = [sc[:SK], sc[SK:]]
                top = jnp.maximum(
                    jnp.max(halves[0], axis=0, keepdims=True) + bias[0],
                    jnp.max(halves[1], axis=0, keepdims=True) + bias[1],
                )
                total = jnp.zeros((1, BLK), jnp.float32)
                for u in range(2):
                    ex = jnp.exp2(halves[u] - jnp.maximum(top, NEG - 2.0 * bias[u]))
                    ebuf[e, s, u * SK:(u + 1) * SK, cols] = ex
                    total += jnp.sum(ex, axis=0, keepdims=True)
                mbuf[e, s, :, cols] = top
                lbuf[e, s, :, cols] = total
            return 0

        lax.fori_loop(0, S, body, 0)

    key_columns(0)
    key_columns(1)
    kc[1].wait_recv()
    kc[2].start()
    kx[1][0].start()
    kc[6].wait_recv()
    kc[5].start()
    kx[6][0].start()
    bc[1].start()
    bc[6].start()
    bx[0][0].start()
    kx[0][1].wait_recv()
    first_pass(0)
    kx[1][1].wait_recv()
    first_pass(1)
    kc[2].wait_recv()
    kc[3].start()
    kx[2][0].start()
    kc[5].wait_recv()
    kc[4].start()
    kx[5][0].start()
    kx[6][1].wait_recv()
    first_pass(6)
    kx[2][1].wait_recv()
    first_pass(2)
    kx[5][1].wait_recv()
    first_pass(5)
    bc[1].wait_recv()
    bc[2].start()
    bx[1][0].start()
    bc[6].wait_recv()
    bc[5].start()
    bx[6][0].start()
    kc[3].wait_recv()
    kx[3][0].start()
    kc[4].wait_recv()
    kx[4][0].start()
    for e in range(2, SLOTS):
        key_columns(e)
    kx[3][1].wait_recv()
    first_pass(3)
    kx[4][1].wait_recv()
    first_pass(4)

    top = mbuf[0]
    for e in range(1, SLOTS):
        top = jnp.maximum(top, mbuf[e])
    total = jnp.zeros_like(top)
    for e in range(SLOTS):
        total += lbuf[e] * jnp.exp2(mbuf[e] - top)
    st[0] = top
    st[1] = total
    stats = [rc(st, str_.at[o], sts.at[o], strs.at[o], peers[o - 1]) for o in range(1, nk)]
    for copy in stats:
        copy.start()
    bc[2].wait_recv()
    bc[3].start()
    bx[2][0].start()
    bc[5].wait_recv()
    bc[4].start()
    bx[5][0].start()
    for copy in stats:
        copy.wait_recv()
    best = top
    for o in range(1, nk):
        best = jnp.maximum(best, str_[o, 0])
    whole = total * jnp.exp2(top - best)
    for o in range(1, nk):
        whole += str_[o, 1] * jnp.exp2(str_[o, 0] - best)
    for e in range(SLOTS):
        fbuf[e] = jnp.exp2(mbuf[e] - best) / whole

    ones = jnp.ones((8, BLK), jnp.float32)

    def second_pass(e):
        def body(s, _):
            bb = bbuf[e, s].reshape(BLK, D)
            bt = bb.T
            kcol = lckb[e, s]
            weights = []
            gathered = jnp.zeros((BLK, BLK), jnp.float32)
            for r in range(RB):
                cols = slice(r * BLK, (r + 1) * BLK)
                prod = nt(bb, c_ref[s, cols, :])
                bias = biases(e, s, r)
                rows = lc_ref[s, pl.ds(qb * RB + r, 1), :]
                spread = jnp.concatenate(
                    [(rows + bias[0]) - kcol[:SK], (rows + bias[1]) - kcol[SK:]], axis=0
                )
                if e == 0:
                    spread = jnp.where(causal(r), spread, NEG)
                decay = jnp.exp(spread)
                mixing = prod * decay
                gap = mixing - ebuf[e, s, :, cols] * fbuf[e, s, :, cols]
                flow = gap * mixing
                w = (gap * decay).astype(jnp.bfloat16)
                weights.append(w)
                gathered += flow
                rf[s, :, cols] += jnp.sum(flow.reshape(BLK // 8, 8, BLK), axis=0)
                gct[s, :, cols] += jnp.dot(bt, w, preferred_element_type=jnp.float32)
            w = jnp.concatenate(weights, axis=1)
            part = jnp.dot(w, c_ref[s], preferred_element_type=jnp.float32)
            colf = nt(ones, gathered, lax.Precision.HIGHEST)[0:1]
            rows = pl.ds(pl.multiple_of(s * SK, SK), SK)
            for u in range(2):
                gp[e, u, rows, :] = part[u * SK:(u + 1) * SK]
            cf[s] = colf
            return 0

        lax.fori_loop(0, S, body, 0)
        for s in range(S):
            for u in range(2):
                gp[e, u, NROW + s:NROW + s + 1, :] = cf[s]

    gx = [rc(gp.at[e, other], sib.at[e], gss.at[e], gsr.at[e], sibling) for e in range(SLOTS)]
    uc = [rc(gp.at[e, core], up.at[i], us.at[i], ur.at[i], prv) for i, e in enumerate((3, 2, 1))]
    dc = [
        rc(gp.at[e, core], dn.at[i], ds.at[i], dr.at[i], to)
        for i, (e, to) in enumerate(((4, nxt), (5, nxt), (6, back)))
    ]

    def grads(e):
        bx[e][1].wait_recv()
        second_pass(e)
        gx[e].start()

    def send_up(i):
        e = 3 - i
        gx[e].wait_recv()
        if i:
            uc[i - 1].wait_recv()
            gp[e, core] = gp[e, core] + sib[e] + up[i - 1]
        else:
            gp[e, core] = gp[e, core] + sib[e]
        uc[i].start()

    def send_dn(i):
        e = 4 + i
        gx[e].wait_recv()
        if i:
            dc[i - 1].wait_recv()
            gp[e, core] = gp[e, core] + sib[e] + dn[i - 1]
        else:
            gp[e, core] = gp[e, core] + sib[e]
        dc[i].start()

    bc[3].wait_recv()
    bx[3][0].start()
    bc[4].wait_recv()
    bx[4][0].start()
    grads(3)
    grads(4)
    send_up(0)
    send_dn(0)
    grads(5)
    grads(2)
    send_dn(1)
    send_up(1)
    grads(6)
    grads(1)
    send_dn(2)
    send_up(2)
    grads(0)

    def spread_c(s, _):
        turned = gct[s].T
        rows = pl.ds(pl.multiple_of(s * SK, SK), SK)
        for o in range(nk):
            gcp[o, rows, :] = turned[o * SK:(o + 1) * SK]
        return 0

    lax.fori_loop(0, S, spread_c, 0)
    for s in range(S):
        flows = jnp.sum(rf[s], axis=0, keepdims=True)
        for o in range(nk):
            g = (o * SK) // BLK
            gcp[o, NROW + s:NROW + s + 1, :] = flows[:, g * BLK:(g + 1) * BLK]
    cc = [
        rc(gcp.at[(kb + o) % nk], gcr.at[o], gcs.at[o], gcrs.at[o], peers[o - 1])
        for o in range(1, nk)
    ]
    for copy in cc:
        copy.start()

    gx[0].wait_recv()
    uc[2].wait_recv()
    dc[2].wait_recv()
    bsum = (gp[0, core] + sib[0]) + (up[2] + dn[2])
    for copy in cc:
        copy.wait_recv()
    csum = gcp[kb]
    for o in range(1, nk):
        csum += gcr[o]
    bsum = bsum * 2.0
    csum = csum * 2.0
    for s in range(S):
        gb_ref[s] = bsum[s * SK:(s + 1) * SK]
        gc_ref[s] = csum[s * SK:(s + 1) * SK]
    rowf = csum[NROW:NROW + S]
    colf = bsum[NROW:NROW + S]
    rowf = jnp.where(jnp.full((S, SK), khalf) == 0, rowf[:, :SK], rowf[:, SK:])
    colf = jnp.where(jnp.full((S, SK), core) == 0, colf[:, :SK], colf[:, SK:])
    gl_ref[...] = rowf - colf

    for e in range(SLOTS):
        kx[e][0].wait_send()
        bx[e][0].wait_send()
        gx[e].wait_send()
        if e:
            kc[e].wait_send()
            bc[e].wait_send()
    for copy in stats + uc + dc + cc:
        copy.wait_send()


def shards(nq, nk, queries, keys, c_proj, b_proj, decay_rate, doc_ids):
    S, R, D = queries.shape
    logcum = jnp.cumsum(-decay_rate, axis=1).reshape(S, -1, BLK)
    pay = S * SK + 8
    vmem = pl.BlockSpec(memory_space=pltpu.VMEM)
    dma = pltpu.SemaphoreType.DMA
    f32, bf16 = jnp.float32, jnp.bfloat16
    return pl.pallas_call(
        functools.partial(kernel, nq, nk),
        out_shape=(
            jax.ShapeDtypeStruct((S, SK, D), f32),
            jax.ShapeDtypeStruct((S, SK, D), f32),
            jax.ShapeDtypeStruct((S, SK), f32),
        ),
        in_specs=[vmem] * 5 + [pl.BlockSpec(memory_space=pltpu.SMEM)],
        out_specs=(vmem, vmem, vmem),
        scratch_shapes=[
            pltpu.VMEM((SLOTS, S, 2, SK, D), bf16),
            pltpu.VMEM((SLOTS, S, 2, SK, D), bf16),
            pltpu.VMEM((SLOTS, S, BLK, R), f32),
            pltpu.VMEM((SLOTS, S, 1, R), f32),
            pltpu.VMEM((SLOTS, S, 1, R), f32),
            pltpu.VMEM((SLOTS, S, 1, R), f32),
            pltpu.VMEM((SLOTS, S, BLK, BLK), f32),
            pltpu.VMEM((S, D, R), f32),
            pltpu.VMEM((S, 8, R), f32),
            pltpu.VMEM((SLOTS, 2, pay, D), f32),
            pltpu.VMEM((SLOTS, pay, D), f32),
            pltpu.VMEM((3, pay, D), f32),
            pltpu.VMEM((3, pay, D), f32),
            pltpu.VMEM((nk, pay, D), f32),
            pltpu.VMEM((nk, pay, D), f32),
            pltpu.VMEM((2, S, 1, R), f32),
            pltpu.VMEM((nk, 2, S, 1, R), f32),
            pltpu.VMEM((S, 1, BLK), f32),
        ]
        + [dma((SLOTS,))] * 8
        + [dma((nk,))] * 2
        + [dma((SLOTS,))] * 2
        + [dma((3,))] * 4
        + [dma((nk,))] * 2,
        compiler_params=pltpu.CompilerParams(
            collective_id=0, has_side_effects=True, vmem_limit_bytes=48 * 1024 * 1024
        ),
    )(queries, c_proj, keys, b_proj, logcum, doc_ids)


def solution(mesh):
    placed = (
        P(None, "qb", None),
        P(None, ("qb", "kb"), None),
        P(None, "qb", None),
        P(None, ("qb", "kb"), None),
        P(),
        P(),
    )
    return jax.shard_map(
        functools.partial(shards, mesh.shape["qb"], mesh.shape["kb"]),
        mesh=mesh,
        in_specs=placed,
        out_specs=(P(None, ("qb", "kb"), None), P(None, ("qb", "kb"), None), P(None, ("qb", "kb"))),
        check_vma=False,
    )
```

time: 644 us -> 83.9 us (0.13)
  the two profiles are of different devices: /device:TPU:1 before, /device:TPU:16 now
where the time goes in v1:
time: 83.9 us; the launch traced here: 83.8 us
  Pallas kernels  78.5 us (94%)
  local copies, waits for them, and re-layouts  2.8 us (3%)
  other arithmetic  1.74 us (2%)
    pallas_call x1, Pallas kernels, shards(): pl.pallas_call(functools.partial(kernel, nq, nk), out_shape=(jax.ShapeDty...  78.5 us
    unnamed x14, local copies, waits for them, and re-layouts  2.53 us

profile of v1, /device:TPU:16, one launch (start us, length us, event | category | flops | bytes accessed | tf_op | source)
XLA Modules:
  0.0 83.8 jit_solution(5810076598280059509)
XLA Ops:
  0.6 1.0 %negate_bitcast_fusion = f32[1,4,128,128]{3,1,2,0:T(4,128)S(1)} fusion(f32[4,16384]{1,0:T(4,128)} %param.10), kind=kLoop, calls=%fused_computation.1 | loop fusion | flops 65536 | bytes 524288
  1.7 0.1 copy.9
  1.8 0.0 copy-start.2
  1.8 0.0 copy-start.3
  1.8 0.3 reduce-window.6
  2.1 0.0 copy-start
  2.1 0.0 copy-start.1
  2.1 0.1 copy.10
  2.3 0.3 reduce-window.9
  2.6 0.0 copy-start.4
  2.6 0.1 broadcast_add_fusion.lc_ref
  2.7 0.0 copy-done.2
  2.7 0.0 copy-done.3
  2.8 0.4 copy-done
  3.2 0.2 copy-done.1
  3.3 0.0 copy-done.4
  3.4 78.5 %shard_map.85 = (f32[4,64,128]{2,1,0:T(8,128)S(1)}, f32[4,64,128]{2,1,0:T(8,128)S(1)}, f32[4,64]{1,0:T(4,128)S(1)}) custom-call(bf16[4,512,128]{2,1,0:T(8,128)(2,1)S(1)} %copy-done, bf16[4,512,128]{2,1,0:T(8,128)(2,1)S(1)} %copy-done.1, bf16[4,64,128]{2,1,0:T(8,128)(2,1)S(1)} %copy-done.2, bf16[4,64,128]{2,1,0:T(8,128)(2,1)S(1)} %copy-done.3, ...), custom_call_target="tpu_custom_call" | custom-call | tf_op jit(solution)/shard_map/pallas_call | solution.py:378
  81.9 0.7 copy.17
  82.5 0.7 copy.18
  83.2 0.6 copy.19
  (3 shorter events, 0.0 us)
Async XLA Ops:
  1.8 0.9 %copy-start.2 = (bf16[4,64,128]{2,1,0:T(8,128)(2,1)S(1)}, bf16[4,64,128]{2,1,0:T(8,128)(2,1)}, u32[]{:S(2)}) copy-start(bf16[4,64,128]{2,1,0:T(8,128)(2,1)} %k_ref.1) | copy-start | bytes 196612
  1.8 0.9 %copy-start.3 = (bf16[4,64,128]{2,1,0:T(8,128)(2,1)S(1)}, bf16[4,64,128]{2,1,0:T(8,128)(2,1)}, u32[]{:S(2)}) copy-start(bf16[4,64,128]{2,1,0:T(8,128)(2,1)} %b_ref.1) | copy-start | bytes 196612
  2.1 1.1 %copy-start = (bf16[4,512,128]{2,1,0:T(8,128)(2,1)S(1)}, bf16[4,512,128]{2,1,0:T(8,128)(2,1)}, u32[]{:S(2)}) copy-start(bf16[4,512,128]{2,1,0:T(8,128)(2,1)} %q_ref.1) | copy-start | bytes 1572868
  2.1 1.2 %copy-start.1 = (bf16[4,512,128]{2,1,0:T(8,128)(2,1)S(1)}, bf16[4,512,128]{2,1,0:T(8,128)(2,1)}, u32[]{:S(2)}) copy-start(bf16[4,512,128]{2,1,0:T(8,128)(2,1)} %c_ref.1) | copy-start | bytes 1572868
  2.6 0.8 copy-start.4

commit v2 on v1

v2 whole, which is shorter than its diff:
```python
import functools
import math

import jax
import jax.numpy as jnp
from jax import lax
from jax.experimental import pallas as pl
from jax.experimental.pallas import tpu as pltpu
from jax.sharding import PartitionSpec as P

MESH = pl.DeviceIdType.MESH
NEG = -1e30
SK = 64
BLK = 128
SLOTS = 7


def nt(a, b, precision=None):
    return lax.dot_general(
        a, b, (((1,), (1,)), ((), ())), preferred_element_type=jnp.float32, precision=precision
    )


def kernel(
    nq, nk,
    q_ref, c_ref, k_ref, b_ref, lc_ref, doc_ref,
    gc_ref, gb_ref, gl_ref,
    kbuf, bbuf, ebuf, mbuf, lbuf, fbuf, lckb, gct, rf, gp, sib, up, dn, gcp, gcr, st, str_,
    ks, kr, bs, br, kss, ksr, bss, bsr, sts, strs, gss, gsr, us, ur, ds, dr, gcs, gcrs,
):
    S, R, D = q_ref.shape
    RB = R // BLK
    HS = S // 2
    NROW = HS * SK
    npair = nq // 2
    qb = lax.axis_index("qb")
    kb = lax.axis_index("kb")
    pr = qb // 2
    core = qb % 2
    other = 1 - core
    kblk = (kb * SK) // BLK
    khalf = kb % 2

    def dev(step):
        return (((pr + step + npair) % npair) * 2 + core, kb)

    nxt, prv, far, back = dev(1), dev(-1), dev(6), dev(-6)
    sibling = (pr * 2 + other, kb)
    peers = [(qb, (kb + o) % nk) for o in range(1, nk)]

    def rc(src, dst, ssem, rsem, to):
        return pltpu.make_async_remote_copy(
            src_ref=src, dst_ref=dst, send_sem=ssem, recv_sem=rsem, device_id=to, device_id_type=MESH
        )

    def ring(own, buf, ssem, rsem):
        def src(e):
            return own if e == 0 else buf.at[e, :, core]

        plan = {1: (0, nxt), 2: (1, nxt), 3: (2, nxt), 6: (0, far), 5: (6, prv), 4: (5, prv)}
        return {e: rc(src(f), buf.at[e, :, core], ssem.at[e], rsem.at[e], to) for e, (f, to) in plan.items()}

    def pair_up(own, buf, ssem, rsem):
        out = []
        for e in range(SLOTS):
            src = own if e == 0 else buf.at[e, :, core]
            out.append((
                rc(src, buf.at[e, :, core], ssem.at[e], rsem.at[e], sibling),
                rc(buf.at[e, :, other], buf.at[e, :, other], ssem.at[e], rsem.at[e], sibling),
            ))
        return out

    kc = ring(k_ref, kbuf, ks, kr)
    bc = ring(b_ref, bbuf, bs, br)
    kx = pair_up(k_ref, kbuf, kss, ksr)
    bx = pair_up(b_ref, bbuf, bss, bsr)

    barrier = pltpu.get_barrier_semaphore()
    partners = [nxt, prv, far, back, sibling] + peers
    for to in partners:
        pl.semaphore_signal(barrier, inc=1, device_id=to, device_id_type=MESH)
    pl.semaphore_wait(barrier, len(partners))

    kc[1].start()
    kc[6].start()
    kx[0][0].start()
    bc[1].start()
    bc[6].start()
    bx[0][0].start()

    lane = lax.broadcasted_iota(jnp.int32, (1, BLK), 1)
    sub = lax.broadcasted_iota(jnp.int32, (BLK, BLK), 0)

    def key_block(e, u):
        j = (pr - e + npair) % npair
        return (2 * j + u) * RB + kblk

    def biases(e, s, r):
        rd = doc_ref[s, qb * RB + r]
        out = []
        for u in range(2):
            kd = doc_ref[s, key_block(e, u)]
            same = kd == rd
            if e:
                same = same & (pr >= e)
            out.append(jnp.where(same, 0.0, NEG).astype(jnp.float32))
        return out

    def causal(r):
        kpos = (2 * pr) * R + kb * SK + jnp.where(sub >= SK, sub - SK + R, sub)
        rpos = qb * R + r * BLK + lane
        return kpos <= rpos

    kbuf[0, :, core] = k_ref[...]
    bbuf[0, :, core] = b_ref[...]
    gct[...] = jnp.zeros_like(gct)
    rf[...] = jnp.zeros_like(rf)
    gp[:, :, :, NROW:, :] = jnp.zeros((SLOTS, 2, 2, 8, D), jnp.float32)
    gcp[:, :, NROW:, :] = jnp.zeros((nk, 2, 8, D), jnp.float32)

    def key_columns(e):
        def body(s, _):
            first = lc_ref[s, pl.ds(key_block(e, 0), 1), :]
            second = lc_ref[s, pl.ds(key_block(e, 1), 1), :]
            low = jnp.concatenate([first[:, :SK], second[:, :SK]], axis=1)
            high = jnp.concatenate([first[:, SK:], second[:, SK:]], axis=1)
            row = jnp.where(jnp.full((1, BLK), khalf) == 0, low, high)
            lckb[e, s] = jnp.broadcast_to(row, (BLK, BLK)).T
            return 0

        lax.fori_loop(0, S, body, 0, unroll=True)

    scale = (D ** -0.5) * math.log2(math.e)

    def first_pass(e):
        def body(s, _):
            every = nt(kbuf[e, s].reshape(BLK, D), q_ref[s]) * scale
            for r in range(RB):
                cols = slice(r * BLK, (r + 1) * BLK)
                sc = every[:, cols]
                if e == 0:
                    sc = jnp.where(causal(r), sc, NEG)
                bias = biases(e, s, r)
                halves = [sc[:SK], sc[SK:]]
                top = jnp.maximum(
                    jnp.max(halves[0], axis=0, keepdims=True) + bias[0],
                    jnp.max(halves[1], axis=0, keepdims=True) + bias[1],
                )
                total = jnp.zeros((1, BLK), jnp.float32)
                for u in range(2):
                    ex = jnp.exp2(halves[u] - jnp.maximum(top, NEG - 2.0 * bias[u]))
                    ebuf[e, s, u * SK:(u + 1) * SK, cols] = ex
                    total += jnp.sum(ex, axis=0, keepdims=True)
                mbuf[e, s, :, cols] = top
                lbuf[e, s, :, cols] = total
            return 0

        lax.fori_loop(0, S, body, 0, unroll=True)

    def passed(copies, siblings, e, follow=None):
        copies[e].wait_recv()
        if follow is not None:
            copies[follow].start()
        siblings[e][0].start()

    def scored(e):
        kx[e][1].wait_recv()
        first_pass(e)

    for e in range(SLOTS):
        key_columns(e)
    scored(0)
    passed(kc, kx, 1, 2)
    passed(bc, bx, 1, 2)
    scored(1)
    passed(kc, kx, 6, 5)
    passed(kc, kx, 2, 3)
    passed(bc, bx, 6, 5)
    passed(bc, bx, 2, 3)
    scored(6)
    scored(2)
    passed(kc, kx, 5, 4)
    passed(kc, kx, 3)
    scored(5)
    scored(3)
    passed(bc, bx, 5, 4)
    passed(bc, bx, 3)
    passed(kc, kx, 4)
    scored(4)

    top = mbuf[0]
    for e in range(1, SLOTS):
        top = jnp.maximum(top, mbuf[e])
    total = jnp.zeros_like(top)
    for e in range(SLOTS):
        total += lbuf[e] * jnp.exp2(mbuf[e] - top)
    st[0] = top
    st[1] = total
    stats = [rc(st, str_.at[o], sts.at[o], strs.at[o], peers[o - 1]) for o in range(1, nk)]
    for copy in stats:
        copy.start()
    passed(bc, bx, 4)
    for copy in stats:
        copy.wait_recv()
    best = top
    for o in range(1, nk):
        best = jnp.maximum(best, str_[o, 0])
    whole = total * jnp.exp2(top - best)
    for o in range(1, nk):
        whole += str_[o, 1] * jnp.exp2(str_[o, 0] - best)
    for e in range(SLOTS):
        fbuf[e] = jnp.exp2(mbuf[e] - best) / whole

    ones = jnp.ones((8, BLK), jnp.float32)

    def second_pass(h, e, i):
        s = h * HS + i
        bb = bbuf[e, s].reshape(BLK, D)
        bt = bb.T
        kcol = lckb[e, s]
        products = nt(bb, c_ref[s])
        weights = []
        gathered = jnp.zeros((BLK, BLK), jnp.float32)
        for r in range(RB):
            cols = slice(r * BLK, (r + 1) * BLK)
            bias = biases(e, s, r)
            rows = lc_ref[s, pl.ds(qb * RB + r, 1), :]
            spread = jnp.concatenate(
                [(rows + bias[0]) - kcol[:SK], (rows + bias[1]) - kcol[SK:]], axis=0
            )
            if e == 0:
                spread = jnp.where(causal(r), spread, NEG)
            decay = jnp.exp(spread)
            mixing = products[:, cols] * decay
            gap = mixing - ebuf[e, s, :, cols] * fbuf[e, s, :, cols]
            flow = gap * mixing
            weights.append((gap * decay).astype(jnp.bfloat16))
            gathered += flow
            rf[s, :, cols] += jnp.sum(flow.reshape(BLK // 8, 8, BLK), axis=0)
        w = jnp.concatenate(weights, axis=1)
        gct[s] += jnp.dot(bt, w, preferred_element_type=jnp.float32)
        part = jnp.dot(w, c_ref[s], preferred_element_type=jnp.float32)
        colf = nt(ones, gathered, lax.Precision.HIGHEST)[0:1]
        for u in range(2):
            gp[e, u, h, i * SK:(i + 1) * SK, :] = part[u * SK:(u + 1) * SK]
            gp[e, u, h, NROW + i:NROW + i + 1, :] = colf

    both = range(2)
    gx = [
        [rc(gp.at[e, other, h], sib.at[e, h], gss.at[e, h], gsr.at[e, h], sibling) for h in both]
        for e in range(SLOTS)
    ]
    uc = [
        [rc(gp.at[e, core, h], up.at[i, h], us.at[i, h], ur.at[i, h], prv) for h in both]
        for i, e in enumerate((3, 2, 1))
    ]
    dc = [
        [rc(gp.at[e, core, h], dn.at[i, h], ds.at[i, h], dr.at[i, h], to) for h in both]
        for i, (e, to) in enumerate(((4, nxt), (5, nxt), (6, back)))
    ]
    cc = [
        [rc(gcp.at[(kb + o) % nk, h], gcr.at[o, h], gcs.at[o, h], gcrs.at[o, h], peers[o - 1]) for h in both]
        for o in range(1, nk)
    ]

    def grads(h, *slots):
        for e in slots:
            if h == 0:
                bx[e][1].wait_recv()
        for e in slots:
            for i in range(HS):
                second_pass(h, e, i)
        for e in slots:
            gx[e][h].start()

    def chain(h, step):
        for e, copies, landed in ((4 + step, dc, dn), (3 - step, uc, up)):
            gx[e][h].wait_recv()
            if step:
                copies[step - 1][h].wait_recv()
                gp[e, core, h] = gp[e, core, h] + sib[e, h] + landed[step - 1, h]
            else:
                gp[e, core, h] = gp[e, core, h] + sib[e, h]
            copies[step][h].start()

    def spread_c(h):
        for i in range(HS):
            s = h * HS + i
            turned = gct[s].T
            flows = jnp.sum(rf[s], axis=0, keepdims=True)
            for o in range(nk):
                g = (o * SK) // BLK
                gcp[o, h, i * SK:(i + 1) * SK, :] = turned[o * SK:(o + 1) * SK]
                gcp[o, h, NROW + i:NROW + i + 1, :] = flows[:, g * BLK:(g + 1) * BLK]
        for copies in cc:
            copies[h].start()

    def finish(h):
        gx[0][h].wait_recv()
        uc[2][h].wait_recv()
        dc[2][h].wait_recv()
        bsum = ((gp[0, core, h] + sib[0, h]) + (up[2, h] + dn[2, h])) * 2.0
        for copies in cc:
            copies[h].wait_recv()
        csum = gcp[kb, h]
        for o in range(1, nk):
            csum += gcr[o, h]
        csum = csum * 2.0
        for i in range(HS):
            s = h * HS + i
            gb_ref[s] = bsum[i * SK:(i + 1) * SK]
            gc_ref[s] = csum[i * SK:(i + 1) * SK]
        rowf = csum[NROW:NROW + HS]
        colf = bsum[NROW:NROW + HS]
        rowf = jnp.where(jnp.full((HS, SK), khalf) == 0, rowf[:, :SK], rowf[:, SK:])
        colf = jnp.where(jnp.full((HS, SK), core) == 0, colf[:, :SK], colf[:, SK:])
        gl_ref[h * HS:(h + 1) * HS] = rowf - colf

    grads(0, 3, 4)
    grads(0, 2, 5)
    chain(0, 0)
    grads(0, 1, 6)
    grads(0, 0)
    spread_c(0)
    grads(1, 3, 4)
    grads(1, 2, 5)
    chain(1, 0)
    chain(0, 1)
    grads(1, 1, 6)
    grads(1, 0)
    spread_c(1)
    chain(1, 1)
    chain(0, 2)
    chain(1, 2)
    finish(0)
    finish(1)

    for e in range(SLOTS):
        kx[e][0].wait_send()
        bx[e][0].wait_send()
        if e:
            kc[e].wait_send()
            bc[e].wait_send()
    for copy in stats:
        copy.wait_send()
    for copies in gx + uc + dc + cc:
        for copy in copies:
            copy.wait_send()


def shards(nq, nk, queries, keys, c_proj, b_proj, decay_rate, doc_ids):
    S, R, D = queries.shape
    logcum = jnp.cumsum(-decay_rate, axis=1).reshape(S, -1, BLK)
    pay = (S // 2) * SK + 8
    vmem = pl.BlockSpec(memory_space=pltpu.VMEM)
    dma = pltpu.SemaphoreType.DMA
    f32, bf16 = jnp.float32, jnp.bfloat16
    return pl.pallas_call(
        functools.partial(kernel, nq, nk),
        out_shape=(
            jax.ShapeDtypeStruct((S, SK, D), f32),
            jax.ShapeDtypeStruct((S, SK, D), f32),
            jax.ShapeDtypeStruct((S, SK), f32),
        ),
        in_specs=[vmem] * 5 + [pl.BlockSpec(memory_space=pltpu.SMEM)],
        out_specs=(vmem, vmem, vmem),
        scratch_shapes=[
            pltpu.VMEM((SLOTS, S, 2, SK, D), bf16),
            pltpu.VMEM((SLOTS, S, 2, SK, D), bf16),
            pltpu.VMEM((SLOTS, S, BLK, R), f32),
            pltpu.VMEM((SLOTS, S, 1, R), f32),
            pltpu.VMEM((SLOTS, S, 1, R), f32),
            pltpu.VMEM((SLOTS, S, 1, R), f32),
            pltpu.VMEM((SLOTS, S, BLK, BLK), f32),
            pltpu.VMEM((S, D, R), f32),
            pltpu.VMEM((S, 8, R), f32),
            pltpu.VMEM((SLOTS, 2, 2, pay, D), f32),
            pltpu.VMEM((SLOTS, 2, pay, D), f32),
            pltpu.VMEM((3, 2, pay, D), f32),
            pltpu.VMEM((3, 2, pay, D), f32),
            pltpu.VMEM((nk, 2, pay, D), f32),
            pltpu.VMEM((nk, 2, pay, D), f32),
            pltpu.VMEM((2, S, 1, R), f32),
            pltpu.VMEM((nk, 2, S, 1, R), f32),
        ]
        + [dma((SLOTS,))] * 8
        + [dma((nk,))] * 2
        + [dma((SLOTS, 2))] * 2
        + [dma((3, 2))] * 4
        + [dma((nk, 2))] * 2,
        compiler_params=pltpu.CompilerParams(
            collective_id=0, has_side_effects=True, vmem_limit_bytes=48 * 1024 * 1024
        ),
    )(queries, c_proj, keys, b_proj, logcum, doc_ids)


def solution(mesh):
    placed = (
        P(None, "qb", None),
        P(None, ("qb", "kb"), None),
        P(None, "qb", None),
        P(None, ("qb", "kb"), None),
        P(),
        P(),
    )
    return jax.shard_map(
        functools.partial(shards, mesh.shape["qb"], mesh.shape["kb"]),
        mesh=mesh,
        in_specs=placed,
        out_specs=(P(None, ("qb", "kb"), None), P(None, ("qb", "kb"), None), P(None, ("qb", "kb"))),
        check_vma=False,
    )
```

time: 83.9 us -> 65.3 us (0.78)
  the two profiles are of different devices: /device:TPU:16 before, /device:TPU:1 now
where the time goes in v2:
time: 65.3 us; the launch traced here: 64.5 us
  Pallas kernels  59.2 us (91%)
  local copies, waits for them, and re-layouts  2.8 us (4%)
  other arithmetic  1.74 us (3%)
  between operations  0.72 us (1%)
    pallas_call x1, Pallas kernels, shards(): pl.pallas_call(functools.partial(kernel, nq, nk), out_shape=(jax.ShapeDty...  59.2 us
    unnamed x14, local copies, waits for them, and re-layouts  2.53 us

profile of v2, /device:TPU:1, one launch (start us, length us, event | category | flops | bytes accessed | tf_op | source)
XLA Modules:
  0.0 64.5 jit_solution(15203126019094096605)
XLA Ops:
  0.6 1.0 %negate_bitcast_fusion = f32[1,4,128,128]{3,1,2,0:T(4,128)S(1)} fusion(f32[4,16384]{1,0:T(4,128)} %param.10), kind=kLoop, calls=%fused_computation.1 | loop fusion | flops 65536 | bytes 524288
  1.7 0.1 copy.9
  1.8 0.0 copy-start.2
  1.8 0.0 copy-start.3
  1.8 0.3 reduce-window.6
  2.1 0.0 copy-start
  2.1 0.0 copy-start.1
  2.1 0.1 copy.10
  2.3 0.3 reduce-window.9
  2.6 0.0 copy-start.4
  2.6 0.1 broadcast_add_fusion.lc_ref
  2.7 0.0 copy-done.2
  2.7 0.0 copy-done.3
  2.8 0.4 copy-done
  3.2 0.2 copy-done.1
  3.3 0.0 copy-done.4
  3.4 59.2 %shard_map.85 = (f32[4,64,128]{2,1,0:T(8,128)S(1)}, f32[4,64,128]{2,1,0:T(8,128)S(1)}, f32[4,64]{1,0:T(4,128)S(1)}) custom-call(bf16[4,512,128]{2,1,0:T(8,128)(2,1)S(1)} %copy-done, bf16[4,512,128]{2,1,0:T(8,128)(2,1)S(1)} %copy-done.1, bf16[4,64,128]{2,1,0:T(8,128)(2,1)S(1)} %copy-done.2, bf16[4,64,128]{2,1,0:T(8,128)(2,1)S(1)} %copy-done.3, ...), custom_call_target="tpu_custom_call" | custom-call | tf_op jit(solution)/shard_map/pallas_call | solution.py:358
  62.6 0.7 %copy.17 = f32[4,64,128]{2,1,0:T(8,128)} copy(f32[4,64,128]{2,1,0:T(8,128)S(1)} %get-tuple-element.6) | data formatting | bytes 262144
  63.2 0.7 %copy.18 = f32[4,64,128]{2,1,0:T(8,128)} copy(f32[4,64,128]{2,1,0:T(8,128)S(1)} %get-tuple-element.7) | data formatting | bytes 262144
  63.9 0.6 copy.19
  (3 shorter events, 0.0 us)
Async XLA Ops:
  1.8 0.9 %copy-start.2 = (bf16[4,64,128]{2,1,0:T(8,128)(2,1)S(1)}, bf16[4,64,128]{2,1,0:T(8,128)(2,1)}, u32[]{:S(2)}) copy-start(bf16[4,64,128]{2,1,0:T(8,128)(2,1)} %k_ref.1) | copy-start | bytes 196612
  1.8 0.9 %copy-start.3 = (bf16[4,64,128]{2,1,0:T(8,128)(2,1)S(1)}, bf16[4,64,128]{2,1,0:T(8,128)(2,1)}, u32[]{:S(2)}) copy-start(bf16[4,64,128]{2,1,0:T(8,128)(2,1)} %b_ref.1) | copy-start | bytes 196612
  2.1 1.1 %copy-start = (bf16[4,512,128]{2,1,0:T(8,128)(2,1)S(1)}, bf16[4,512,128]{2,1,0:T(8,128)(2,1)}, u32[]{:S(2)}) copy-start(bf16[4,512,128]{2,1,0:T(8,128)(2,1)} %q_ref.1) | copy-start | bytes 1572868
  2.1 1.2 %copy-start.1 = (bf16[4,512,128]{2,1,0:T(8,128)(2,1)S(1)}, bf16[4,512,128]{2,1,0:T(8,128)(2,1)}, u32[]{:S(2)}) copy-start(bf16[4,512,128]{2,1,0:T(8,128)(2,1)} %c_ref.1) | copy-start | bytes 1572868
  2.6 0.8 %copy-start.4 = (s32[4,128]{1,0:T(4,128)S(1)}, s32[4,128]{1,0:T(4,128)}, u32[]{:S(2)}) copy-start(s32[4,128]{1,0:T(4,128)} %doc_ref.1) | copy-start | bytes 6148

commit v3 on v2

v3 whole, which is shorter than its diff:
```python
import functools
import math

import jax
import jax.numpy as jnp
from jax import lax
from jax.experimental import pallas as pl
from jax.experimental.pallas import tpu as pltpu
from jax.sharding import PartitionSpec as P

MESH = pl.DeviceIdType.MESH
HIGHEST = lax.Precision.HIGHEST
NEG = -1e30
SK = 64
BLK = 128
SLOTS = 7
WAVES = 2


def nt(a, b, precision=None):
    return lax.dot_general(
        a, b, (((1,), (1,)), ((), ())), preferred_element_type=jnp.float32, precision=precision
    )


def kernel(
    nq, nk,
    q_ref, c_ref, k_ref, b_ref, rate_ref, doc_ref,
    gc_ref, gb_ref, gl_ref,
    qbuf, cbuf, kbuf, bbuf, ebuf, mbuf, lbuf, fbuf, lcs, lckb, gct, rf, gp, up, dn, gcp, gcr, st, str_, fin, got, held,
    ks, kr, bs, br, qs, qr, cs, cr, hs, hr, sts, strs, us, ur, ds, dr, gcs, gcrs, fs, fr,
):
    S, R, D = q_ref.shape
    RB = R // BLK
    NB = nq * RB
    RR = 2 * R
    nx = nk // 2
    npair = nq // 2
    qb = lax.axis_index("qb")
    kb = lax.axis_index("kb")
    pr = qb // 2
    core = qb % 2
    other = 1 - core
    kx = kb // 2
    ky = kb % 2
    both = range(2)
    me = 2 * ky + core

    def side(g):
        return ky if g == 0 else 1 - ky

    def dev(step, which, g=0):
        return (((pr + step + npair) % npair) * 2 + which, kx * 2 + side(g))

    sibling = dev(0, other)
    crowd = [(dx, g) for dx in range(nx) for g in both if dx or g]

    def peer(dx, g):
        return (qb, ((kx + dx) % nx) * 2 + side(g))

    barrier = pltpu.get_barrier_semaphore()
    partners = [dev(step, u, g) for step in (1, -1, 6, -6) for u in both for g in both]
    partners += [sibling, dev(0, other, 1)] + [peer(dx, g) for dx, g in crowd]
    for to in partners:
        pl.semaphore_signal(barrier, inc=1, device_id=to, device_id_type=MESH)

    def rc(src, dst, ssem, rsem, to):
        return pltpu.make_async_remote_copy(
            src_ref=src, dst_ref=dst, send_sem=ssem, recv_sem=rsem, device_id=to, device_id_type=MESH
        )

    def own_push(own, buf, ssem, rsem):
        push, land = {}, {}
        for e in (0, 1, 6):
            for g in both:
                push[e, g], land[e, g] = [], []
                for v in both:
                    if e == g == v == 0:
                        continue
                    which = (core + v) % 2
                    push[e, g].append(rc(
                        own.at[2 * side(g) + which], buf.at[e, g, core],
                        ssem.at[e, g, v], rsem.at[e, g, v], dev(e, which, g),
                    ))
                    land[e, g].append(rc(
                        buf.at[e, g, which], buf.at[e, g, which],
                        ssem.at[e, g, v], rsem.at[e, g, v], dev(-e, which, g),
                    ))
        return push, land

    def pass_on(buf, ssem, rsem):
        out = {}
        for e, f, step in ((2, 1, 1), (3, 2, 1), (5, 6, -1), (4, 5, -1)):
            for g in both:
                out[e, g] = rc(
                    buf.at[f, g], buf.at[e, g], ssem.at[e, g, 0], rsem.at[e, g, 0], dev(step, core)
                )
        return out

    def swap(own, buf, ssem, rsem):
        return (
            rc(own.at[2 * ky + other], buf.at[core], ssem, rsem, sibling),
            rc(buf.at[other], buf.at[other], ssem, rsem, sibling),
        )

    kp, kl = own_push(k_ref, kbuf, ks, kr)
    bp, bl = own_push(b_ref, bbuf, bs, br)
    kf, bf = pass_on(kbuf, ks, kr), pass_on(bbuf, bs, br)
    qx = swap(q_ref, qbuf, qs, qr)
    cx = swap(c_ref, cbuf, cs, cr)

    lane = lax.broadcasted_iota(jnp.int32, (1, BLK), 1)
    sub = lax.broadcasted_iota(jnp.int32, (BLK, BLK), 0)

    def key_block(e, g, u):
        j = (pr - e + npair) % npair
        return (2 * j + u) * RB + ((kx * 2 + side(g)) * SK) // BLK

    def key_columns(e, w):
        first = lcs[pl.ds(key_block(e, w, 0), 1), :]
        second = lcs[pl.ds(key_block(e, w, 1), 1), :]
        low = jnp.concatenate([first[:, :SK], second[:, :SK]], axis=1)
        high = jnp.concatenate([first[:, SK:], second[:, SK:]], axis=1)
        row = jnp.where(jnp.full((1, BLK), side(w)) == 0, low, high)
        lckb[e, w] = jnp.broadcast_to(row, (BLK, BLK)).T

    kbuf[0, 0, core] = k_ref[me]
    bbuf[0, 0, core] = b_ref[me]
    pl.semaphore_wait(barrier, len(partners))

    def push(copies, e, w):
        for copy in copies[e, w]:
            copy.start()

    for g in both:
        push(kp, 6, g)
    for g in both:
        push(kp, 1, g)
    for g in both:
        push(kp, 0, g)
    qx[0].start()
    for g in both:
        push(bp, 6, g)
    for g in both:
        push(bp, 1, g)
    for g in both:
        push(bp, 0, g)
    cx[0].start()

    rates = rate_ref[me]
    row = lax.broadcasted_iota(jnp.int32, (BLK, BLK), 0)
    col = lax.broadcasted_iota(jnp.int32, (BLK, BLK), 1)
    within = jnp.dot(
        rates, (row <= col).astype(jnp.float32), preferred_element_type=jnp.float32, precision=HIGHEST
    )
    row = lax.broadcasted_iota(jnp.int32, (NB, NB), 0)
    col = lax.broadcasted_iota(jnp.int32, (NB, NB), 1)
    base = pr * 2 * RB
    after = ((col >= base) & (col < row)).astype(jnp.float32)
    before = ((col >= row) & (col < base)).astype(jnp.float32)
    blocks = jnp.dot(
        after - before, rates, preferred_element_type=jnp.float32, precision=HIGHEST
    )
    lcs[...] = -(within + jnp.sum(blocks, axis=1, keepdims=True))

    for e in range(SLOTS):
        for w in range(WAVES):
            key_columns(e, w)

    qbuf[core] = q_ref[me]
    cbuf[core] = c_ref[me]
    gct[...] = jnp.zeros_like(gct)
    rf[...] = jnp.zeros_like(rf)
    gp[:, :, BLK:, :] = jnp.zeros((SLOTS, WAVES, 8, D), jnp.float32)
    gcp[:, BLK:, :] = jnp.zeros((nk, 8, D), jnp.float32)
    fin[:, :, BLK:, :] = jnp.zeros((WAVES, 2, 8, D), jnp.float32)

    def biases(e, w, r):
        rd = doc_ref[me, pr * 2 * RB + r]
        out = []
        for u in range(2):
            same = doc_ref[me, key_block(e, w, u)] == rd
            if e:
                same = same & (pr >= e)
            out.append(jnp.where(same, 0.0, NEG).astype(jnp.float32))
        return out

    def causal(w, r):
        kpos = (2 * pr) * R + (kx * 2 + side(w)) * SK + jnp.where(sub >= SK, sub - SK + R, sub)
        rpos = pr * RR + r * BLK + lane
        return kpos <= rpos

    scale = (D ** -0.5) * math.log2(math.e)

    def first_pass(e, w):
        every = nt(kbuf[e, w].reshape(BLK, D), qbuf[...].reshape(RR, D)) * scale
        for r in range(2 * RB):
            cols = slice(r * BLK, (r + 1) * BLK)
            sc = every[:, cols]
            if e == 0:
                sc = jnp.where(causal(w, r), sc, NEG)
            bias = biases(e, w, r)
            halves = [sc[:SK], sc[SK:]]
            top = jnp.maximum(
                jnp.max(halves[0], axis=0, keepdims=True) + bias[0],
                jnp.max(halves[1], axis=0, keepdims=True) + bias[1],
            )
            total = jnp.zeros((1, BLK), jnp.float32)
            for u in range(2):
                ex = jnp.exp2(halves[u] - jnp.maximum(top, NEG - 2.0 * bias[u]))
                ebuf[e, w, u * SK:(u + 1) * SK, cols] = ex
                total += jnp.sum(ex, axis=0, keepdims=True)
            mbuf[e, w, :, cols] = top
            lbuf[e, w, :, cols] = total

    def passed(w, *slots):
        for land, forward in ((kl, kf), (bl, bf)):
            for e in slots:
                if e in (0, 1, 6):
                    for copy in land[e, w]:
                        copy.wait_recv()
                else:
                    forward[e, w].wait_recv()
                follow = {1: 2, 2: 3, 6: 5, 5: 4}.get(e)
                if follow is not None:
                    forward[follow, w].start()

    stats = [rc(st, str_.at[o], sts.at[o], strs.at[o], peer(o, 0)) for o in range(1, nx)]
    every = [(e, w) for e in range(SLOTS) for w in both]

    for w in both:
        for copy in kl[0, w]:
            copy.wait_recv()
    qx[1].wait_recv()
    for w in both:
        first_pass(0, w)
    for w in both:
        passed(w, 1, 6)
        first_pass(1, w)
        first_pass(6, w)
    for w in both:
        passed(w, 2, 5)
        first_pass(2, w)
        first_pass(5, w)
    for w in both:
        kf[3, w].wait_recv()
        kf[4, w].wait_recv()
        first_pass(3, w)
        first_pass(4, w)
    top = mbuf[0, 0]
    for at in every:
        top = jnp.maximum(top, mbuf[at])
    total = jnp.zeros_like(top)
    for at in every:
        total += lbuf[at] * jnp.exp2(mbuf[at] - top)
    st[0] = top
    st[1] = total
    for copy in stats:
        copy.start()
    for w in both:
        for copy in bl[0, w]:
            copy.wait_recv()
        for e in (3, 4):
            bf[e, w].wait_recv()
    cx[1].wait_recv()
    for copy in stats:
        copy.wait_recv()
    best = top
    for o in range(1, nx):
        best = jnp.maximum(best, str_[o, 0])
    whole = total * jnp.exp2(top - best)
    for o in range(1, nx):
        whole += str_[o, 1] * jnp.exp2(str_[o, 0] - best)
    for at in every:
        fbuf[at] = jnp.exp2(mbuf[at] - best) / whole

    ones = jnp.ones((8, BLK), jnp.float32)

    def second_pass(e, w):
        bb = bbuf[e, w].reshape(BLK, D)
        bt = bb.T
        kcol = lckb[e, w]
        crows = cbuf[...].reshape(RR, D)
        products = nt(bb, crows)
        weights = []
        gathered = jnp.zeros((BLK, BLK), jnp.float32)
        for r in range(2 * RB):
            cols = slice(r * BLK, (r + 1) * BLK)
            bias = biases(e, w, r)
            rows = lcs[pl.ds(pr * 2 * RB + r, 1), :]
            spread = jnp.concatenate(
                [(rows + bias[0]) - kcol[:SK], (rows + bias[1]) - kcol[SK:]], axis=0
            )
            if e == 0:
                spread = jnp.where(causal(w, r), spread, NEG)
            decay = jnp.exp(spread)
            mixing = products[:, cols] * decay
            gap = mixing - ebuf[e, w, :, cols] * fbuf[e, w, :, cols]
            flow = gap * mixing
            weights.append((gap * decay).astype(jnp.bfloat16))
            gathered += flow
            rf[:, cols] += jnp.sum(flow.reshape(BLK // 8, 8, BLK), axis=0)
        wide = jnp.concatenate(weights, axis=1)
        gct[...] += jnp.dot(bt, wide, preferred_element_type=jnp.float32)
        gp[e, w, :BLK, :] = jnp.dot(wide, crows, preferred_element_type=jnp.float32)
        gp[e, w, BLK:BLK + 1, :] = nt(ones, gathered, HIGHEST)[0:1]

    uc = [
        [
            rc(gp.at[e, w], up.at[i, w], us.at[i, w], ur.at[i, w], dev(-1, core, w if e == 1 else 0))
            for w in both
        ]
        for i, e in enumerate((3, 2, 1))
    ]
    dc = [
        [
            rc(
                gp.at[e, w], dn.at[i, w], ds.at[i, w], dr.at[i, w],
                dev(-6, core, w) if e == 6 else dev(1, core),
            )
            for w in both
        ]
        for i, e in enumerate((4, 5, 6))
    ]
    cc = {
        (dx, g): rc(
            gcp.at[((kx + dx) % nx) * 2 + side(g)], gcr.at[dx, g],
            gcs.at[dx, g], gcrs.at[dx, g], peer(dx, g),
        )
        for dx, g in crowd
    }
    fx = [rc(fin.at[w, other], got.at[w], fs.at[w], fr.at[w], sibling) for w in both]
    hx = rc(gp.at[0, 1], held, hs, hr, dev(0, core, 1))

    def chain(w, step):
        for e, copies, landed in ((4 + step, dc, dn), (3 - step, uc, up)):
            if step:
                copies[step - 1][w].wait_recv()
                gp[e, w] = gp[e, w] + landed[step - 1, w]
            copies[step][w].start()

    def finish(w):
        uc[2][w].wait_recv()
        dc[2][w].wait_recv()
        if w:
            hx.wait_recv()
            bsum = held[...]
        else:
            bsum = gp[0, 0]
        bsum = (bsum + (up[2, w] + dn[2, w])) * 2.0
        for dx in range(nx):
            if dx or w:
                cc[dx, w].wait_recv()
        csum = gcr[0, 1] if w else gcp[kb]
        for dx in range(1, nx):
            csum += gcr[dx, w]
        csum = csum * 2.0
        flows = []
        for u in range(2):
            fin[w, u, :SK, :] = bsum[u * SK:(u + 1) * SK]
            fin[w, u, SK:BLK, :] = csum[u * SK:(u + 1) * SK]
            rowf = csum[BLK + u:BLK + u + 1]
            rowf = jnp.where(jnp.full((1, SK), ky) == 0, rowf[:, :SK], rowf[:, SK:])
            flows.append(rowf - bsum[BLK:BLK + 1, u * SK:(u + 1) * SK])
        flows = jnp.concatenate(flows, axis=1)
        for u in range(2):
            fin[w, u, BLK:BLK + 1, :] = flows
        fx[w].start()
        gb_ref[2 * side(w) + core] = fin[w, core, :SK, :]
        gc_ref[2 * side(w) + core] = fin[w, core, SK:BLK, :]

    for w in both:
        second_pass(3, w)
        second_pass(4, w)
        chain(w, 0)
    for w in both:
        second_pass(2, w)
        second_pass(5, w)
    for w in both:
        second_pass(1, w)
        second_pass(6, w)
        chain(w, 1)
    second_pass(0, 1)
    hx.start()
    second_pass(0, 0)
    turned = gct[...].T
    flows = jnp.sum(rf[...], axis=0, keepdims=True)
    for o in range(nk):
        for u in range(2):
            at = u * R + o * SK
            gcp[o, u * SK:(u + 1) * SK, :] = turned[at:at + SK]
            at = u * R + (o * SK) // BLK * BLK
            gcp[o, BLK + u:BLK + u + 1, :] = flows[:, at:at + BLK]
    for at in sorted(cc, key=lambda at: -at[1]):
        cc[at].start()
    chain(0, 2)
    chain(1, 2)
    finish(0)
    finish(1)

    for w in both:
        fx[w].wait_recv()
        gb_ref[2 * side(w) + other] = got[w, :SK, :]
        gc_ref[2 * side(w) + other] = got[w, SK:BLK, :]

    def pick(flag, a, b):
        return jnp.where(jnp.full((1, BLK), flag) == 0, a, b)

    ours = [fin[w, core, BLK:BLK + 1, :] for w in both]
    rest = [got[w, BLK:BLK + 1, :] for w in both]
    ours = [pick(ky, ours[0], ours[1]), pick(ky, ours[1], ours[0])]
    rest = [pick(ky, rest[0], rest[1]), pick(ky, rest[1], rest[0])]
    flows = jnp.concatenate(
        [pick(core, x, y) for y_hi in both for x, y in ((ours[y_hi], rest[y_hi]), (rest[y_hi], ours[y_hi]))],
        axis=0,
    )
    gl_ref[...] = jnp.where(jnp.full((S, SK), core) == 0, flows[:, :SK], flows[:, SK:])

    for copies in list(kp.values()) + list(bp.values()) + uc + dc:
        for copy in copies:
            copy.wait_send()
    for copy in list(kf.values()) + list(bf.values()) + stats + list(cc.values()) + fx:
        copy.wait_send()
    for copy in (qx[0], cx[0], hx):
        copy.wait_send()


def shards(nq, nk, queries, keys, c_proj, b_proj, decay_rate, doc_ids):
    S, R, D = queries.shape
    rates = decay_rate.reshape(S, -1, BLK)
    NB = rates.shape[1]
    RR = 2 * R
    pay = BLK + 8
    vmem = pl.BlockSpec(memory_space=pltpu.VMEM)
    dma = pltpu.SemaphoreType.DMA
    f32, bf16 = jnp.float32, jnp.bfloat16
    return pl.pallas_call(
        functools.partial(kernel, nq, nk),
        out_shape=(
            jax.ShapeDtypeStruct((S, SK, D), f32),
            jax.ShapeDtypeStruct((S, SK, D), f32),
            jax.ShapeDtypeStruct((S, SK), f32),
        ),
        in_specs=[vmem] * 5 + [pl.BlockSpec(memory_space=pltpu.SMEM)],
        out_specs=(vmem, vmem, vmem),
        scratch_shapes=[
            pltpu.VMEM((2, R, D), bf16),
            pltpu.VMEM((2, R, D), bf16),
            pltpu.VMEM((SLOTS, WAVES, 2, SK, D), bf16),
            pltpu.VMEM((SLOTS, WAVES, 2, SK, D), bf16),
            pltpu.VMEM((SLOTS, WAVES, BLK, RR), f32),
            pltpu.VMEM((SLOTS, WAVES, 1, RR), f32),
            pltpu.VMEM((SLOTS, WAVES, 1, RR), f32),
            pltpu.VMEM((SLOTS, WAVES, 1, RR), f32),
            pltpu.VMEM((NB, BLK), f32),
            pltpu.VMEM((SLOTS, WAVES, BLK, BLK), f32),
            pltpu.VMEM((D, RR), f32),
            pltpu.VMEM((8, RR), f32),
            pltpu.VMEM((SLOTS, WAVES, pay, D), f32),
            pltpu.VMEM((3, WAVES, pay, D), f32),
            pltpu.VMEM((3, WAVES, pay, D), f32),
            pltpu.VMEM((nk, pay, D), f32),
            pltpu.VMEM((nk // 2, 2, pay, D), f32),
            pltpu.VMEM((2, 1, RR), f32),
            pltpu.VMEM((nk // 2, 2, 1, RR), f32),
            pltpu.VMEM((WAVES, 2, pay, D), f32),
            pltpu.VMEM((WAVES, pay, D), f32),
            pltpu.VMEM((pay, D), f32),
        ]
        + [dma((SLOTS, WAVES, 2))] * 4
        + [dma] * 6
        + [dma((nk // 2,))] * 2
        + [dma((3, WAVES))] * 4
        + [dma((nk // 2, 2))] * 2
        + [dma((WAVES,))] * 2,
        compiler_params=pltpu.CompilerParams(
            collective_id=0, has_side_effects=True, vmem_limit_bytes=48 * 1024 * 1024
        ),
    )(queries, c_proj, keys, b_proj, rates, doc_ids)


def solution(mesh):
    placed = (
        P(None, "qb", None),
        P(None, ("qb", "kb"), None),
        P(None, "qb", None),
        P(None, ("qb", "kb"), None),
        P(),
        P(),
    )
    return jax.shard_map(
        functools.partial(shards, mesh.shape["qb"], mesh.shape["kb"]),
        mesh=mesh,
        in_specs=placed,
        out_specs=(P(None, ("qb", "kb"), None), P(None, ("qb", "kb"), None), P(None, ("qb", "kb"))),
        check_vma=False,
    )
```

time: 65.3 us -> 61.7 us (0.945)
  Pallas kernels: 59.2 us -> 55.1 us
  local copies, waits for them, and re-layouts: 2.8 us -> 5.71 us
  other arithmetic: 1.74 us -> 0 us
    pallas_call x1, Pallas kernels: 59.2 us -> 55.1 us  [shards(): pl.pallas_call(functools.partial(kernel, nq, nk), out_shape=(jax.ShapeDty...]
    unnamed x14, local copies, waits for them, and re-layouts: 2.53 us -> 5.71 us
    unnamed x1 -> x0, other arithmetic: 1.01 us -> none
    another operation x3 -> x0, other arithmetic: 0.73 us -> none
where the time goes in v3:
time: 61.7 us; the launch traced here: 61.5 us
  Pallas kernels  55.1 us (89%)
  local copies, waits for them, and re-layouts  5.71 us (9%)
  between operations  0.66 us (1%)
    pallas_call x1, Pallas kernels, shards(): pl.pallas_call(functools.partial(kernel, nq, nk), out_shape=(jax.ShapeDty...  55.1 us
    unnamed x14, local copies, waits for them, and re-layouts  5.71 us

profile of v3, /device:TPU:1, one launch (start us, length us, event | category | flops | bytes accessed | tf_op | source)
XLA Modules:
  0.0 61.5 jit_solution(17908408961945700308)
XLA Ops:
  0.6 0.0 copy-start
  0.6 0.0 copy-start.4
  0.7 1.0 %copy.11 = f32[1,4,128,128]{3,2,1,0:T(8,128)S(1)} copy(f32[1,4,128,128]{3,1,2,0:T(4,128)} %bitcast.5) | data formatting | bytes 524288
  1.7 0.1 copy-done
  1.8 0.0 copy-done.4
  1.8 0.0 copy-start.1
  1.8 1.0 %copy-done.1 = bf16[4,512,128]{2,1,0:T(8,128)(2,1)S(1)} copy-done((bf16[4,512,128]{2,1,0:T(8,128)(2,1)S(1)}, bf16[4,512,128]{2,1,0:T(8,128)(2,1)}, u32[]{:S(2)}) %copy-start.1) | copy-done | bytes 524312
  2.8 0.0 copy-start.2
  2.8 0.8 %copy-done.2 = bf16[4,64,128]{2,1,0:T(8,128)(2,1)S(1)} copy-done((bf16[4,64,128]{2,1,0:T(8,128)(2,1)S(1)}, bf16[4,64,128]{2,1,0:T(8,128)(2,1)}, u32[]{:S(2)}) %copy-start.2) | copy-done | bytes 65560
  3.6 0.0 copy-start.3
  3.6 0.8 %copy-done.3 = bf16[4,64,128]{2,1,0:T(8,128)(2,1)S(1)} copy-done((bf16[4,64,128]{2,1,0:T(8,128)(2,1)S(1)}, bf16[4,64,128]{2,1,0:T(8,128)(2,1)}, u32[]{:S(2)}) %copy-start.3) | copy-done | bytes 65560
  4.5 55.1 %shard_map.85 = (f32[4,64,128]{2,1,0:T(8,128)S(1)}, f32[4,64,128]{2,1,0:T(8,128)S(1)}, f32[4,64]{1,0:T(4,128)S(1)}) custom-call(bf16[4,512,128]{2,1,0:T(8,128)(2,1)S(1)} %copy-done, bf16[4,512,128]{2,1,0:T(8,128)(2,1)S(1)} %copy-done.1, bf16[4,64,128]{2,1,0:T(8,128)(2,1)S(1)} %copy-done.2, bf16[4,64,128]{2,1,0:T(8,128)(2,1)S(1)} %copy-done.3, ...), custom_call_target="tpu_custom_call" | custom-call | tf_op jit(solution)/shard_map/pallas_call | solution.py:437
  59.6 0.7 %copy.15 = f32[4,64,128]{2,1,0:T(8,128)} copy(f32[4,64,128]{2,1,0:T(8,128)S(1)} %get-tuple-element.6) | data formatting | bytes 262144
  60.2 0.7 %copy.16 = f32[4,64,128]{2,1,0:T(8,128)} copy(f32[4,64,128]{2,1,0:T(8,128)S(1)} %get-tuple-element.7) | data formatting | bytes 262144
  60.9 0.6 copy.17
Async XLA Ops:
  0.6 1.1 %copy-start = (bf16[4,512,128]{2,1,0:T(8,128)(2,1)S(1)}, bf16[4,512,128]{2,1,0:T(8,128)(2,1)}, u32[]{:S(2)}) copy-start(bf16[4,512,128]{2,1,0:T(8,128)(2,1)} %q_ref.1) | copy-start | bytes 1572868
  0.6 1.1 %copy-start.4 = (s32[4,128]{1,0:T(4,128)S(1)}, s32[4,128]{1,0:T(4,128)}, u32[]{:S(2)}) copy-start(s32[4,128]{1,0:T(4,128)} %doc_ref.1) | copy-start | bytes 6148
  1.8 1.0 %copy-start.1 = (bf16[4,512,128]{2,1,0:T(8,128)(2,1)S(1)}, bf16[4,512,128]{2,1,0:T(8,128)(2,1)}, u32[]{:S(2)}) copy-start(bf16[4,512,128]{2,1,0:T(8,128)(2,1)} %c_ref.1) | copy-start | bytes 1572868
  2.8 0.8 %copy-start.2 = (bf16[4,64,128]{2,1,0:T(8,128)(2,1)S(1)}, bf16[4,64,128]{2,1,0:T(8,128)(2,1)}, u32[]{:S(2)}) copy-start(bf16[4,64,128]{2,1,0:T(8,128)(2,1)} %k_ref.1) | copy-start | bytes 196612
  3.6 0.8 %copy-start.3 = (bf16[4,64,128]{2,1,0:T(8,128)(2,1)S(1)}, bf16[4,64,128]{2,1,0:T(8,128)(2,1)}, u32[]{:S(2)}) copy-start(bf16[4,64,128]{2,1,0:T(8,128)(2,1)} %b_ref.1) | copy-start | bytes 196612

commit v4 on v3

--- a/solution.py
+++ b/solution.py
@@ -27,8 +27,8 @@
     nq, nk,
     q_ref, c_ref, k_ref, b_ref, rate_ref, doc_ref,
     gc_ref, gb_ref, gl_ref,
-    qbuf, cbuf, kbuf, bbuf, ebuf, mbuf, lbuf, fbuf, lcs, lckb, gct, rf, gp, up, dn, gcp, gcr, st, str_, fin, got, held,
-    ks, kr, bs, br, qs, qr, cs, cr, hs, hr, sts, strs, us, ur, ds, dr, gcs, gcrs, fs, fr,
+    qbuf, cbuf, kbuf, bbuf, ebuf, mbuf, lbuf, fbuf, lcs, lckb, gct, rf, gp, up, dn, gcp, gcr, st, str_, fin, got, held, rbuf, mixbuf, decbuf,
+    ls, ks, kr, bs, br, qs, qr, cs, cr, hs, hr, sts, strs, us, ur, ds, dr, gcs, gcrs, fs, fr,
 ):
     S, R, D = q_ref.shape
     RB = R // BLK
@@ -109,6 +109,19 @@
     qx = swap(q_ref, qbuf, qs, qr)
     cx = swap(c_ref, cbuf, cs, cr)
 
+    local = [
+        pltpu.make_async_copy(src, dst, ls.at[i])
+        for i, (src, dst) in enumerate((
+            (k_ref.at[me], kbuf.at[0, 0, core]),
+            (q_ref.at[me], qbuf.at[core]),
+            (rate_ref, rbuf),
+            (b_ref.at[me], bbuf.at[0, 0, core]),
+            (c_ref.at[me], cbuf.at[core]),
+        ))
+    ]
+    for copy in local:
+        copy.start()
+
     lane = lax.broadcasted_iota(jnp.int32, (1, BLK), 1)
     sub = lax.broadcasted_iota(jnp.int32, (BLK, BLK), 0)
 
@@ -124,8 +137,6 @@
         row = jnp.where(jnp.full((1, BLK), side(w)) == 0, low, high)
         lckb[e, w] = jnp.broadcast_to(row, (BLK, BLK)).T
 
-    kbuf[0, 0, core] = k_ref[me]
-    bbuf[0, 0, core] = b_ref[me]
     pl.semaphore_wait(barrier, len(partners))
 
     def push(copies, e, w):
@@ -147,28 +158,32 @@
         push(bp, 0, g)
     cx[0].start()
 
-    rates = rate_ref[me]
+    local[2].wait()
+    row = lax.broadcasted_iota(jnp.int32, (NB, NB * S), 0)
+    col = lax.broadcasted_iota(jnp.int32, (NB, NB * S), 1)
+    ours = (col % S) == me
+    blk = col // S
+    base = pr * 2 * RB
+    rates = jnp.dot(
+        (ours & (blk == row)).astype(jnp.float32), rbuf[...],
+        preferred_element_type=jnp.float32, precision=HIGHEST,
+    )
+    after = (ours & (blk >= base) & (blk < row)).astype(jnp.float32)
+    before = (ours & (blk >= row) & (blk < base)).astype(jnp.float32)
+    blocks = jnp.dot(
+        after - before, rbuf[...], preferred_element_type=jnp.float32, precision=HIGHEST
+    )
     row = lax.broadcasted_iota(jnp.int32, (BLK, BLK), 0)
     col = lax.broadcasted_iota(jnp.int32, (BLK, BLK), 1)
     within = jnp.dot(
         rates, (row <= col).astype(jnp.float32), preferred_element_type=jnp.float32, precision=HIGHEST
     )
-    row = lax.broadcasted_iota(jnp.int32, (NB, NB), 0)
-    col = lax.broadcasted_iota(jnp.int32, (NB, NB), 1)
-    base = pr * 2 * RB
-    after = ((col >= base) & (col < row)).astype(jnp.float32)
-    before = ((col >= row) & (col < base)).astype(jnp.float32)
-    blocks = jnp.dot(
-        after - before, rates, preferred_element_type=jnp.float32, precision=HIGHEST
-    )
     lcs[...] = -(within + jnp.sum(blocks, axis=1, keepdims=True))
 
     for e in range(SLOTS):
         for w in range(WAVES):
             key_columns(e, w)
 
-    qbuf[core] = q_ref[me]
-    cbuf[core] = c_ref[me]
     gct[...] = jnp.zeros_like(gct)
     rf[...] = jnp.zeros_like(rf)
     gp[:, :, BLK:, :] = jnp.zeros((SLOTS, WAVES, 8, D), jnp.float32)
@@ -213,6 +228,22 @@
             mbuf[e, w, :, cols] = top
             lbuf[e, w, :, cols] = total
 
+    def mix_pass(e, w):
+        kcol = lckb[e, w]
+        products = nt(bbuf[e, w].reshape(BLK, D), cbuf[...].reshape(RR, D))
+        for r in range(2 * RB):
+            cols = slice(r * BLK, (r + 1) * BLK)
+            bias = biases(e, w, r)
+            rows = lcs[pl.ds(pr * 2 * RB + r, 1), :]
+            spread = jnp.concatenate(
+                [(rows + bias[0]) - kcol[:SK], (rows + bias[1]) - kcol[SK:]], axis=0
+            )
+            if e == 0:
+                spread = jnp.where(causal(w, r), spread, NEG)
+            decay = jnp.exp(spread)
+            decbuf[e, w, :, cols] = decay
+            mixbuf[e, w, :, cols] = products[:, cols] * decay
+
     def passed(w, *slots):
         for land, forward in ((kl, kf), (bl, bf)):
             for e in slots:
@@ -232,16 +263,31 @@
         for copy in kl[0, w]:
             copy.wait_recv()
     qx[1].wait_recv()
+    local[0].wait()
+    local[1].wait()
     for w in both:
         first_pass(0, w)
     for w in both:
         passed(w, 1, 6)
+    for w in both:
         first_pass(1, w)
         first_pass(6, w)
     for w in both:
+        for copy in bl[0, w]:
+            copy.wait_recv()
+    cx[1].wait_recv()
+    local[3].wait()
+    local[4].wait()
+    mix_pass(0, 0)
+    mix_pass(0, 1)
+    for w in both:
         passed(w, 2, 5)
+    for w in both:
         first_pass(2, w)
         first_pass(5, w)
+    for w in both:
+        mix_pass(1, w)
+        mix_pass(6, w)
     for w in both:
         kf[3, w].wait_recv()
         kf[4, w].wait_recv()
@@ -258,11 +304,12 @@
     for copy in stats:
         copy.start()
     for w in both:
-        for copy in bl[0, w]:
-            copy.wait_recv()
         for e in (3, 4):
             bf[e, w].wait_recv()
-    cx[1].wait_recv()
+            mix_pass(e, w)
+    for w in both:
+        mix_pass(2, w)
+        mix_pass(5, w)
     for copy in stats:
         copy.wait_recv()
     best = top
@@ -277,32 +324,20 @@
     ones = jnp.ones((8, BLK), jnp.float32)
 
     def second_pass(e, w):
-        bb = bbuf[e, w].reshape(BLK, D)
-        bt = bb.T
-        kcol = lckb[e, w]
-        crows = cbuf[...].reshape(RR, D)
-        products = nt(bb, crows)
+        bt = bbuf[e, w].reshape(BLK, D).T
         weights = []
         gathered = jnp.zeros((BLK, BLK), jnp.float32)
         for r in range(2 * RB):
             cols = slice(r * BLK, (r + 1) * BLK)
-            bias = biases(e, w, r)
-            rows = lcs[pl.ds(pr * 2 * RB + r, 1), :]
-            spread = jnp.concatenate(
-                [(rows + bias[0]) - kcol[:SK], (rows + bias[1]) - kcol[SK:]], axis=0
-            )
-            if e == 0:
-                spread = jnp.where(causal(w, r), spread, NEG)
-            decay = jnp.exp(spread)
-            mixing = products[:, cols] * decay
+            mixing = mixbuf[e, w, :, cols]
             gap = mixing - ebuf[e, w, :, cols] * fbuf[e, w, :, cols]
             flow = gap * mixing
-            weights.append((gap * decay).astype(jnp.bfloat16))
+            weights.append((gap * decbuf[e, w, :, cols]).astype(jnp.bfloat16))
             gathered += flow
             rf[:, cols] += jnp.sum(flow.reshape(BLK // 8, 8, BLK), axis=0)
         wide = jnp.concatenate(weights, axis=1)
         gct[...] += jnp.dot(bt, wide, preferred_element_type=jnp.float32)
-        gp[e, w, :BLK, :] = jnp.dot(wide, crows, preferred_element_type=jnp.float32)
+        gp[e, w, :BLK, :] = jnp.dot(wide, cbuf[...].reshape(RR, D), preferred_element_type=jnp.float32)
         gp[e, w, BLK:BLK + 1, :] = nt(ones, gathered, HIGHEST)[0:1]
 
     uc = [
@@ -427,8 +462,8 @@
 
 def shards(nq, nk, queries, keys, c_proj, b_proj, decay_rate, doc_ids):
     S, R, D = queries.shape
-    rates = decay_rate.reshape(S, -1, BLK)
-    NB = rates.shape[1]
+    NB = decay_rate.shape[1] // BLK
+    rates = decay_rate.reshape(S, NB, BLK).transpose(1, 0, 2).reshape(NB * S, BLK)
     RR = 2 * R
     pay = BLK + 8
     vmem = pl.BlockSpec(memory_space=pltpu.VMEM)
@@ -441,7 +476,7 @@
             jax.ShapeDtypeStruct((S, SK, D), f32),
             jax.ShapeDtypeStruct((S, SK), f32),
         ),
-        in_specs=[vmem] * 5 + [pl.BlockSpec(memory_space=pltpu.SMEM)],
+        in_specs=[pl.BlockSpec(memory_space=pltpu.HBM)] * 5 + [pl.BlockSpec(memory_space=pltpu.SMEM)],
         out_specs=(vmem, vmem, vmem),
         scratch_shapes=[
             pltpu.VMEM((2, R, D), bf16),
@@ -466,7 +501,11 @@
             pltpu.VMEM((WAVES, 2, pay, D), f32),
             pltpu.VMEM((WAVES, pay, D), f32),
             pltpu.VMEM((pay, D), f32),
+            pltpu.VMEM((NB * S, BLK), f32),
+            pltpu.VMEM((SLOTS, WAVES, BLK, RR), f32),
+            pltpu.VMEM((SLOTS, WAVES, BLK, RR), f32),
         ]
+        + [dma((5,))]
         + [dma((SLOTS, WAVES, 2))] * 4
         + [dma] * 6
         + [dma((nk // 2,))] * 2
@@ -474,7 +513,7 @@
         + [dma((nk // 2, 2))] * 2
         + [dma((WAVES,))] * 2,
         compiler_params=pltpu.CompilerParams(
-            collective_id=0, has_side_effects=True, vmem_limit_bytes=48 * 1024 * 1024
+            collective_id=0, has_side_effects=True, vmem_limit_bytes=63 * 1024 * 1024
         ),
     )(queries, c_proj, keys, b_proj, rates, doc_ids)
 

time: 61.7 us -> 59.6 us (0.966)
  local copies, waits for them, and re-layouts: 5.71 us -> 2.86 us
  Pallas kernels: 55.1 us -> 56 us
    unnamed x14 -> x7, local copies, waits for them, and re-layouts: 5.71 us -> 2.86 us
    pallas_call x1, Pallas kernels: 55.1 us -> 56 us  [shards(): pl.pallas_call(functools.partial(kernel, nq, nk), out_shape=(jax.ShapeDty...]
where the time goes in v4:
time: 59.6 us; the launch traced here: 59.5 us
  Pallas kernels  56 us (94%)
  local copies, waits for them, and re-layouts  2.86 us (5%)
  between operations  0.65 us (1%)
    pallas_call x1, Pallas kernels, shards(): pl.pallas_call(functools.partial(kernel, nq, nk), out_shape=(jax.ShapeDty...  56 us
    unnamed x7, local copies, waits for them, and re-layouts  2.86 us

profile of v4, /device:TPU:1, one launch (start us, length us, event | category | flops | bytes accessed | tf_op | source)
XLA Modules:
  0.0 59.5 jit_solution(5565658179903494744)
XLA Ops:
  0.6 56.0 %shard_map.85 = (f32[4,64,128]{2,1,0:T(8,128)}, f32[4,64,128]{2,1,0:T(8,128)}, f32[4,64]{1,0:T(4,128)}) custom-call(bf16[4,512,128]{2,1,0:T(8,128)(2,1)} %q_ref.1, bf16[4,512,128]{2,1,0:T(8,128)(2,1)} %c_ref.1, bf16[4,64,128]{2,1,0:T(8,128)(2,1)} %k_ref.1, bf16[4,64,128]{2,1,0:T(8,128)(2,1)} %b_ref.1, f32[512,128]{1,0:T(8,128)} %bitcast.5, s32[4,128]{1,0:T(4,128)} %doc_ref.1), custom_call_target="tpu_custom_call" | custom-call | tf_op jit(solution)/shard_map/pallas_call | solution.py:472
  56.6 0.0 copy-start
  56.6 1.6 %copy.13 = f32[4,64,128]{2,1,0:T(8,128)} copy(f32[4,64,128]{2,1,0:T(8,128)} %get-tuple-element.6) | data formatting | bytes 262144
  58.2 0.0 copy-done
  58.2 0.0 copy-start.1
  58.2 0.7 %copy.14 = f32[4,64,128]{2,1,0:T(8,128)} copy(f32[4,64,128]{2,1,0:T(8,128)S(1)} %copy-done) | data formatting | bytes 262144
  58.9 0.0 copy-done.1
  58.9 0.6 copy.15
Async XLA Ops:
  56.6 1.6 %copy-start = (f32[4,64,128]{2,1,0:T(8,128)S(1)}, f32[4,64,128]{2,1,0:T(8,128)}, u32[]{:S(2)}) copy-start(f32[4,64,128]{2,1,0:T(8,128)} %get-tuple-element.7) | copy-start | bytes 393220
  58.2 0.7 %copy-start.1 = (f32[4,64]{1,0:T(4,128)S(1)}, f32[4,64]{1,0:T(4,128)}, u32[]{:S(2)}) copy-start(f32[4,64]{1,0:T(4,128)} %get-tuple-element.8) | copy-start | bytes 3076

commit v5 on v4

--- a/solution.py
+++ b/solution.py
@@ -244,8 +244,8 @@
             decbuf[e, w, :, cols] = decay
             mixbuf[e, w, :, cols] = products[:, cols] * decay
 
-    def passed(w, *slots):
-        for land, forward in ((kl, kf), (bl, bf)):
+    def passed(land, forward, *slots):
+        for w in both:
             for e in slots:
                 if e in (0, 1, 6):
                     for copy in land[e, w]:
@@ -267,32 +267,27 @@
     local[1].wait()
     for w in both:
         first_pass(0, w)
-    for w in both:
-        passed(w, 1, 6)
-    for w in both:
-        first_pass(1, w)
-        first_pass(6, w)
-    for w in both:
-        for copy in bl[0, w]:
-            copy.wait_recv()
+    passed(kl, kf, 1, 6)
+    for e in (1, 6):
+        for w in both:
+            first_pass(e, w)
+    passed(bl, bf, 1, 6)
+    passed(bl, bf, 0)
     cx[1].wait_recv()
     local[3].wait()
     local[4].wait()
-    mix_pass(0, 0)
-    mix_pass(0, 1)
-    for w in both:
-        passed(w, 2, 5)
-    for w in both:
-        first_pass(2, w)
-        first_pass(5, w)
-    for w in both:
-        mix_pass(1, w)
-        mix_pass(6, w)
-    for w in both:
-        kf[3, w].wait_recv()
-        kf[4, w].wait_recv()
-        first_pass(3, w)
-        first_pass(4, w)
+    passed(kl, kf, 2, 5)
+    for e in (2, 5):
+        for w in both:
+            first_pass(e, w)
+    passed(bl, bf, 2, 5)
+    for e in (0, 1, 6):
+        for w in both:
+            mix_pass(e, w)
+    passed(kl, kf, 3, 4)
+    for e in (3, 4):
+        for w in both:
+            first_pass(e, w)
     top = mbuf[0, 0]
     for at in every:
         top = jnp.maximum(top, mbuf[at])
@@ -367,12 +362,17 @@
     fx = [rc(fin.at[w, other], got.at[w], fs.at[w], fr.at[w], sibling) for w in both]
     hx = rc(gp.at[0, 1], held, hs, hr, dev(0, core, 1))
 
-    def chain(w, step):
-        for e, copies, landed in ((4 + step, dc, dn), (3 - step, uc, up)):
-            if step:
-                copies[step - 1][w].wait_recv()
-                gp[e, w] = gp[e, w] + landed[step - 1, w]
-            copies[step][w].start()
+    def chain(e, copies, landed, w, step):
+        if step:
+            copies[step - 1][w].wait_recv()
+            gp[e, w] = gp[e, w] + landed[step - 1, w]
+        copies[step][w].start()
+
+    def send_dn(w, step):
+        chain(4 + step, dc, dn, w, step)
+
+    def send_up(w, step):
+        chain(3 - step, uc, up, w, step)
 
     def finish(w):
         uc[2][w].wait_recv()
@@ -405,16 +405,19 @@
         gc_ref[2 * side(w) + core] = fin[w, core, SK:BLK, :]
 
     for w in both:
+        second_pass(4, w)
+        send_dn(w, 0)
+    for w in both:
         second_pass(3, w)
-        second_pass(4, w)
-        chain(w, 0)
-    for w in both:
-        second_pass(2, w)
-        second_pass(5, w)
-    for w in both:
+        send_up(w, 0)
+    for e in (5, 2, 6):
+        for w in both:
+            second_pass(e, w)
+    for w in both:
+        send_dn(w, 1)
         second_pass(1, w)
-        second_pass(6, w)
-        chain(w, 1)
+    for w in both:
+        send_up(w, 1)
     second_pass(0, 1)
     hx.start()
     second_pass(0, 0)
@@ -428,8 +431,10 @@
             gcp[o, BLK + u:BLK + u + 1, :] = flows[:, at:at + BLK]
     for at in sorted(cc, key=lambda at: -at[1]):
         cc[at].start()
-    chain(0, 2)
-    chain(1, 2)
+    for w in both:
+        send_dn(w, 2)
+    for w in both:
+        send_up(w, 2)
     finish(0)
     finish(1)
 

time: 59.6 us -> 59.2 us (level)
  no operation moved by 1% of the time
where the time goes in v5:
time: 59.2 us; the launch traced here: 59 us
  Pallas kernels  55.5 us (94%)
  local copies, waits for them, and re-layouts  2.86 us (5%)
  between operations  0.65 us (1%)
    pallas_call x1, Pallas kernels, shards(): pl.pallas_call(functools.partial(kernel, nq, nk), out_shape=(jax.ShapeDty...  55.5 us
    unnamed x7, local copies, waits for them, and re-layouts  2.86 us

profile of v5, /device:TPU:1, one launch (start us, length us, event | category | flops | bytes accessed | tf_op | source)
XLA Modules:
  0.0 59.0 jit_solution(5441371045073864014)
XLA Ops:
  0.6 55.5 %shard_map.85 = (f32[4,64,128]{2,1,0:T(8,128)}, f32[4,64,128]{2,1,0:T(8,128)}, f32[4,64]{1,0:T(4,128)}) custom-call(bf16[4,512,128]{2,1,0:T(8,128)(2,1)} %q_ref.1, bf16[4,512,128]{2,1,0:T(8,128)(2,1)} %c_ref.1, bf16[4,64,128]{2,1,0:T(8,128)(2,1)} %k_ref.1, bf16[4,64,128]{2,1,0:T(8,128)(2,1)} %b_ref.1, f32[512,128]{1,0:T(8,128)} %bitcast.5, s32[4,128]{1,0:T(4,128)} %doc_ref.1), custom_call_target="tpu_custom_call" | custom-call | tf_op jit(solution)/shard_map/pallas_call | solution.py:477
  56.2 0.0 copy-start
  56.2 1.6 %copy.13 = f32[4,64,128]{2,1,0:T(8,128)} copy(f32[4,64,128]{2,1,0:T(8,128)} %get-tuple-element.6) | data formatting | bytes 262144
  57.8 0.0 copy-done
  57.8 0.0 copy-start.1
  57.8 0.7 %copy.14 = f32[4,64,128]{2,1,0:T(8,128)} copy(f32[4,64,128]{2,1,0:T(8,128)S(1)} %copy-done) | data formatting | bytes 262144
  58.4 0.0 copy-done.1
  58.5 0.6 copy.15
Async XLA Ops:
  56.2 1.6 %copy-start = (f32[4,64,128]{2,1,0:T(8,128)S(1)}, f32[4,64,128]{2,1,0:T(8,128)}, u32[]{:S(2)}) copy-start(f32[4,64,128]{2,1,0:T(8,128)} %get-tuple-element.7) | copy-start | bytes 393220
  57.8 0.7 %copy-start.1 = (f32[4,64]{1,0:T(4,128)S(1)}, f32[4,64]{1,0:T(4,128)}, u32[]{:S(2)}) copy-start(f32[4,64]{1,0:T(4,128)} %get-tuple-element.8) | copy-start | bytes 3076
